TPU v7x, 256 devices: a whole 4x4x8 slice. The times are simulated.
256 devices in a mesh: index: 128 (over z, x_hi, y, core), rep: 2 (over x_lo).
Axes of the slice: x: 4 (x_hi: 2, x_lo: 2; x = x_hi * 2 + x_lo), y: 4, z: 8, core: 2. Of those that a mesh axis runs over, the one named last changes fastest.
Arguments:
- queries: bfloat16 [128, 2, 8, 16, 512], P('index', 'rep'), may hold values from -6 to 6
- database: bfloat16 [512, 8, 16, 512], P('index'), may hold values from -6 to 6
- db_frames: int32 [512], P('index'), may hold values from 1 to 8
- cand_shard: int32 [128, 2, 128, 1], P('index', 'rep'), may hold values from 0 to 127; in each aligned block of 128 rows (0 to 127, 128 to 255, ..., all dimensions but the last counted through in order) at most 2 rows name the same one
- cand_local: int32 [128, 2, 128], P('index', 'rep'), may hold values from 0 to 3
- conv_one: float32 [3, 3, 1, 32], replicated, may hold values from -2 to 2
- conv_two: float32 [3, 3, 32, 64], replicated, may hold values from -0.375 to 0.375
- conv_three: float32 [3, 3, 64, 128], replicated, may hold values from -0.25 to 0.25
- conv_out: float32 [128], replicated, may hold values from -0.5 to 0.5
Outputs:
- coarse: float32 [2, 128, 512], P('rep', None, 'index')
- refined: float32 [128, 2, 128], P('index', 'rep')
Inputs may be any that keep to these rules, and one draw needn't show every extreme that they name: `cand_shard`: among the 128 candidates of one query no shard is named more than 2 times, and some query names one shard exactly 2 times; a few shards are named far more often than others.
All inputs are finite; a program needn't handle non-finite values.
Results may differ from a plain program's by a relative error of at most 0.0003.
Values may be sent and summed in bfloat16 or wider, within the bound.
A program may use at most 128 MiB of HBM per device.

v0:
```python
import math

import jax
import jax.numpy as jnp
from jax import lax
from jax.sharding import PartitionSpec as P

HIGH = lax.Precision.HIGHEST


def block_frame_maps(query_block, clips):
    block_count, frame_count, region_count, feature_width = query_block.shape
    clip_count = clips.shape[0]
    clip_rows = clips.reshape(clip_count * frame_count * region_count, feature_width)
    query_cols = jnp.transpose(query_block, (2, 0, 1, 3)).reshape(
        region_count * block_count * frame_count, feature_width
    )
    similar = jnp.dot(
        clip_rows, query_cols.T, preferred_element_type=jnp.float32
    ) * feature_width ** (-0.5)
    similar = similar.reshape(
        clip_count, frame_count, region_count, region_count, block_count * frame_count
    )
    region_best = jnp.max(similar, axis=2)
    frame_map = jnp.mean(region_best, axis=2)
    frame_map = frame_map.reshape(clip_count, frame_count, block_count, frame_count)
    return jnp.transpose(frame_map, (2, 0, 3, 1))


def chamfer(frame_map, lengths):
    frame_count = frame_map.shape[-1]
    present = jnp.arange(frame_count)[None, None, :] < lengths[:, None, None]
    masked = jnp.where(present, frame_map, -jnp.inf)
    return jnp.mean(jnp.max(masked, axis=2), axis=1)


def convolve(inputs, kernel):
    return lax.conv_general_dilated(
        inputs, kernel, (1, 1), "SAME", dimension_numbers=("NHWC", "HWIO", "NHWC"), precision=HIGH
    )


def network_score(frame_map, lengths, conv_one, conv_two, conv_three, conv_out):
    frame_count = frame_map.shape[-1]
    present = jnp.arange(frame_count)[None, None, :] < lengths[:, None, None]
    inputs = jnp.where(present, frame_map, 0.0)[..., None]
    hidden = jax.nn.relu(convolve(inputs, conv_one))
    hidden = jax.nn.relu(convolve(hidden, conv_two))
    hidden = jax.nn.relu(convolve(hidden, conv_three))
    output_map = jnp.einsum("bfgc,c->bfg", hidden, conv_out, precision=HIGH)
    return chamfer(output_map, lengths)


def local(
    queries, database, db_frames, cand_shard, cand_local, conv_one, conv_two, conv_three, conv_out
):
    shard_total = lax.axis_size("index")
    cand_total = cand_local.shape[2]
    slot_total = max(2, 2 * cand_total // shard_total)
    clip_total, frame_count, region_count, feature_width = database.shape
    owners = cand_shard[0, 0, :, 0]
    local_ids = cand_local[0, 0]
    same_owner = owners[:, None] == owners[None, :]
    earlier = jnp.arange(cand_total)[None, :] < jnp.arange(cand_total)[:, None]
    slot_rank = jnp.sum(same_owner & earlier, axis=1)
    matches = (owners[:, None, None] == jnp.arange(shard_total)[None, :, None]) & (
        slot_rank[:, None, None] == jnp.arange(slot_total)[None, None, :]
    )
    wanted_ids = jnp.sum(jnp.where(matches, local_ids[:, None, None], 0), axis=0)
    received_ids = lax.all_to_all(wanted_ids, "index", split_axis=0, concat_axis=0, tiled=True)
    piece = lax.all_gather(queries[:, 0], "index", axis=0, tiled=True)
    row_count = piece.shape[0]
    group_size = math.gcd(row_count, 8)
    grouped = piece.reshape(
        row_count // group_size, group_size, frame_count, region_count, feature_width
    )
    all_maps = lax.map(lambda block: block_frame_maps(block, database), grouped)
    all_maps = all_maps.reshape(row_count, clip_total, frame_count, frame_count)
    row_scores = jax.vmap(lambda one_map: chamfer(one_map, db_frames))(all_maps)
    coarse_part = row_scores
    selector = (received_ids[..., None] == jnp.arange(clip_total)[None, None, :]).astype(
        jnp.float32
    )
    picked = jnp.einsum("nsv,nvfg->nsfg", selector, all_maps, precision=HIGH)
    held_maps = picked
    coarse_part, held_maps = (coarse_part, held_maps)
    held_lengths = jnp.take(db_frames, received_ids.reshape(-1), axis=0).reshape(
        shard_total, slot_total
    )
    slot_scores = network_score(
        held_maps.reshape(-1, frame_count, frame_count),
        held_lengths.reshape(-1),
        conv_one,
        conv_two,
        conv_three,
        conv_out,
    )
    returned = lax.all_to_all(
        slot_scores.reshape(shard_total, slot_total),
        "index",
        split_axis=0,
        concat_axis=0,
        tiled=True,
    )
    refined = jnp.sum(jnp.where(matches, returned[None], 0.0), axis=(1, 2))
    return (coarse_part[None], refined[None, None])


def solution(mesh):
    in_specs = (
        P("index", "rep", None, None, None),
        P("index", None, None, None),
        P("index"),
        P("index", "rep", None, None),
        P("index", "rep", None),
        P(),
        P(),
        P(),
        P(),
    )
    out_specs = (P("rep", None, "index"), P("index", "rep", None))
    return jax.shard_map(local, mesh=mesh, in_specs=in_specs, out_specs=out_specs, check_vma=False)
```

profile of v0, /device:TPU:1, one launch (start us, length us, event | category | flops | bytes accessed | tf_op | source)
XLA Modules:
  0.0 493.0 jit_solution(1948896323367453647)
XLA Ops:
  11.1 16.4 %all-to-all-start = ((s32[128,1,2]{2,1,0:T(1,128)}), s32[128,1,2]{2,1,0:T(1,128)S(1)}, u32[]{:S(2)}, u32[]{:S(2)}) async-start(s32[128,1,2]{2,1,0:T(1,128)} %copy.65), calls=%async_computation | async-start | bytes 131072 | tf_op jit(solution)/shard_map/all_to_all | solution.py:70
  29.7 9.9 %all-to-all-done = s32[128,1,2]{2,1,0:T(1,128)S(1)} async-done(((s32[128,1,2]{2,1,0:T(1,128)}), s32[128,1,2]{2,1,0:T(1,128)S(1)}, u32[]{:S(2)}, u32[]{:S(2)}) %all-to-all-start) | async-done | bytes 1056 | tf_op jit(solution)/shard_map/all_to_all | solution.py:70
  43.9 124.0 %all-gather.3.cloned.1.call-done = bf16[128,1,8,16,512]{4,3,2,1,0:T(8,128)(2,1)} async-done(((bf16[1,1,8,16,512]{4,3,2,1,0:T(8,128)(2,1)}), bf16[128,1,8,16,512]{4,3,2,1,0:T(8,128)(2,1)}) %all-gather.3.cloned.1.call-update) | async-done | bytes 16777232 | tf_op jit(solution)/shard_map/all_gather | solution.py:71
  167.9 193.4 %while.10 = (s32[]{:T(128)}, f32[16,8,4,8,8]{4,3,2,1,0:T(8,128)}, bf16[16,8,8,16,512]{4,3,2,1,0:T(8,128)(2,1)}, bf16[4,8,16,512]{3,2,1,0:T(8,128)(2,1)}, s32[]{:T(128)}, /*index=5*/f32[]{:T(128)}, f32[]{:T(128)}) while((s32[]{:T(128)}, f32[16,8,4,8,8]{4,3,2,1,0:T(8,128)}, bf16[16,8,8,16,512]{4,3,2,1,0:T(8,128)(2,1)}, ...), condition=%wide.region_3.4_spmd, body=%wide.region_0.3_spmd.sunk | while | flops 537919488 | bytes 20906112 | solution.py:77
  176.4 2.6 reduce_max.32
  188.5 2.6 reduce_max.32
  200.5 2.6 reduce_max.32
  212.6 2.6 reduce_max.32
  224.6 2.6 reduce_max.32
  236.7 2.6 reduce_max.32
  248.8 2.6 reduce_max.32
  260.9 2.6 reduce_max.32
  272.9 2.6 reduce_max.32
  285.0 2.6 reduce_max.32
  297.1 2.6 reduce_max.32
  309.1 2.6 reduce_max.32
  321.2 2.6 reduce_max.32
  333.3 2.6 reduce_max.32
  345.3 2.6 reduce_max.32
  369.4 10.7 %fusion.8 = f32[256,8,8,64]{0,3,2,1:T(8,128)S(1)} fusion(f32[3,3,32,64]{3,2,1,0:T(8,128)S(1)} %copy-done.3, f32[256,8,8,32]{0,3,2,1:T(8,128)S(1)} %fusion.24), kind=kOutput, calls=%fused_computation.12 | convolution fusion | flops 3045588992 | bytes 6365184 | tf_op jit(solution)/shard_map/conv_general_dilated | solution.py:38
  380.0 76.3 %fusion.3 = f32[256,8,8,128]{3,0,2,1:T(8,128)S(1)} fusion(f32[3,3,64,128]{3,2,1,0:T(8,128)S(1)} %copy-done, f32[256,8,8,64]{0,3,2,1:T(8,128)S(1)} %fusion.8), kind=kOutput, calls=%fused_computation.7 | convolution fusion | flops 12181307392 | bytes 12877824 | tf_op jit(solution)/shard_map/conv_general_dilated | solution.py:38
  456.4 7.3 %fusion = f32[1,256,8,8]{1,0,3,2:T(1,128)S(1)} fusion(f32[256,8,8,128]{3,0,2,1:T(8,128)S(1)} %fusion.3, f32[128]{0:T(128)S(1)} %copy-done.5), kind=kOutput, calls=%fused_computation.4 | convolution fusion | flops 27262976 | bytes 8454656 | tf_op jit(solution)/shard_map/bfgc,c->bfg/dot_general | solution.py:50
  464.4 8.6 %all-to-all-start.1 = ((f32[128,1,2]{2,1,0:T(1,128)}), f32[128,1,2]{2,1,0:T(1,128)S(1)}, u32[]{:S(2)}, u32[]{:S(2)}) async-start(f32[128,1,2]{2,1,0:T(1,128)} %bitcast.24), calls=%async_computation.1 | async-start | bytes 131072 | tf_op jit(solution)/shard_map/all_to_all | solution.py:98
  473.9 11.3 %all-to-all-done.1 = f32[128,1,2]{2,1,0:T(1,128)S(1)} async-done(((f32[128,1,2]{2,1,0:T(1,128)}), f32[128,1,2]{2,1,0:T(1,128)S(1)}, u32[]{:S(2)}, u32[]{:S(2)}) %all-to-all-start.1) | async-done | bytes 1056 | tf_op jit(solution)/shard_map/all_to_all | solution.py:98
  (238 shorter events, 173.7 us)
Async XLA Ops:
  7.2 372.9 %copy-start = (f32[3,3,64,128]{3,2,1,0:T(8,128)S(1)}, f32[3,3,64,128]{3,2,1,0:T(8,128)}, u32[]{:S(2)}) copy-start(f32[3,3,64,128]{3,2,1,0:T(8,128)} %param.18) | copy-start | bytes 884740
  7.2 160.7 %all-gather.3.cloned.1.call-start = ((), (), s32[]{:S(2)}) async-start(), calls=%async_computation.2 | async-start | bytes 16908288 | tf_op jit(solution)/shard_map/all_gather | solution.py:71
  11.1 28.5 %all-to-all-start = ((s32[128,1,2]{2,1,0:T(1,128)}), s32[128,1,2]{2,1,0:T(1,128)S(1)}, u32[]{:S(2)}, u32[]{:S(2)}) async-start(s32[128,1,2]{2,1,0:T(1,128)} %copy.65), calls=%async_computation | async-start | bytes 131072 | tf_op jit(solution)/shard_map/all_to_all | solution.py:70
  167.9 2.0 copy-start.1
  179.9 2.0 copy-start.1
  192.0 2.0 copy-start.1
  204.1 2.0 copy-start.1
  216.1 2.0 copy-start.1
  228.2 2.0 copy-start.1
  240.3 2.0 copy-start.1
  252.3 2.0 copy-start.1
  264.4 2.0 copy-start.1
  276.5 2.0 copy-start.1
  288.5 2.0 copy-start.1
  300.6 2.0 copy-start.1
  312.7 2.0 copy-start.1
  324.8 2.0 copy-start.1
  336.8 2.0 copy-start.1
  348.9 2.0 copy-start.1
  361.3 2.8 copy-start.2
  366.6 0.7 copy-start.4
  366.7 2.6 copy-start.3
  380.0 76.3 %copy-start.5 = (f32[128]{0:T(128)S(1)}, f32[128]{0:T(128)}, u32[]{:S(2)}) copy-start(f32[128]{0:T(128)} %param.19) | copy-start | bytes 1540
  464.4 20.7 %all-to-all-start.1 = ((f32[128,1,2]{2,1,0:T(1,128)}), f32[128,1,2]{2,1,0:T(1,128)S(1)}, u32[]{:S(2)}, u32[]{:S(2)}) async-start(f32[128,1,2]{2,1,0:T(1,128)} %bitcast.24), calls=%async_computation.1 | async-start | bytes 131072 | tf_op jit(solution)/shard_map/all_to_all | solution.py:98
Sparse Core Ops, SparseCore 0:
  11.6 156.2 all-gather.2
where the time goes:
time: 494 us; the launch traced here: 493 us
  waiting for transfers between devices  146 us (30%)
  matrix products  132 us (27%)
  local copies, waits for them, and re-layouts  122 us (25%)
  other arithmetic  52.4 us (11%)
  starting transfers between devices  25.1 us (5%)
  between operations  14.5 us (3%)
    all_gather x1, waiting for transfers between devices, local(): piece = lax.all_gather(queries[:, 0], 'index', axis=0, tiled=True)  124 us
    conv_general_dilated x3, matrix products, convolve(): lax.conv_general_dilated(inputs, kernel, (1, 1), 'SAME', dimension_number...  89 us
    reduce_max x16, other arithmetic, block_frame_maps(): region_best = jnp.max(similar, axis=2)  41.5 us
    reshape x16, local copies, waits for them, and re-layouts, block_frame_maps(): similar.reshape(clip_count, frame_count, region_count, region_count, bloc...  40.1 us
    dot_general x16, matrix products, block_frame_maps(): jnp.dot(clip_rows, query_cols.T, preferred_element_type=jnp.float32)  33.5 us
    dynamic_slice x32, local copies, waits for them, and re-layouts, local(): all_maps = lax.map(lambda block: block_frame_maps(block, database), grouped)  31.4 us
    mul x16, local copies, waits for them, and re-layouts, block_frame_maps(): jnp.dot(clip_rows, query_cols.T, preferred_element_type=jnp.float32)  30.7 us
    all_to_all x1, starting transfers between devices, local(): lax.all_to_all(wanted_ids, 'index', split_axis=0, concat_axis=0, tiled=True)  16.4 us
  transfers between devices with their start and end apart: 3, of which 3 were waited for; matrix products, arithmetic and copies ran while one was open for 2% of the time, Pallas kernels for 0%

commit v1 on v0

v1 whole, which is shorter than its diff:
```python
import functools

import jax
import jax.numpy as jnp
from jax import lax
from jax.experimental import pallas as pl
from jax.experimental.pallas import tpu as pltpu
from jax.sharding import PartitionSpec as P

MESH = pl.DeviceIdType.MESH
F32, BF16 = jnp.float32, jnp.bfloat16
ABSENT = -(2.0 ** 100)
K = 512


def dot(a, b):
    return jnp.dot(a, b, preferred_element_type=F32)


def iota(shape, axis):
    return lax.broadcasted_iota(jnp.int32, shape, axis)


def halves(x):
    high = x.astype(BF16)
    return high, (x - high.astype(F32)).astype(BF16)


def thirds(x):
    high, rest = x.astype(BF16), None
    rest = x - high.astype(F32)
    mid = rest.astype(BF16)
    return high, mid, (rest - mid.astype(F32)).astype(BF16)


def pick(onehot, x):
    y = dot(onehot, jnp.concatenate(thirds(x), axis=1))
    n = x.shape[1]
    return y[:, :n] + (y[:, n:2 * n] + y[:, 2 * n:])


def kernel(
    q_hbm, db_hbm, frames, shard_hbm, local_hbm, one_hbm, two_hbm, three_hbm, out_hbm,
    coarse_ref, refined_ref,
    qbuf, dbraw, dbp, fmap, lens, msg, rbuf, cbuf, perm, fold,
    shard_v, local_v, one_v, two_v, three_v, out_v,
    w1, w2, w3h, w3l, x1, x2h, x2l, pen, best,
    send_sem, recv_sem, msg_send, msg_recv, local_sem,
):
    index, rep = lax.axis_index("index"), lax.axis_index("rep")
    c, y, xh, z = index % 2, (index // 2) % 4, (index // 8) % 2, index // 16
    x = xh * 2 + rep
    a, b = y // 2, ((y + 1) // 2) % 2
    ell = rep

    def device(z, x, y, c):
        return (((z * 2 + x // 2) * 4 + y) * 2 + c, x % 2)

    def y_of(a, b):
        return a * 3 + b * (1 - 2 * a)

    me_q = z * 4 + a * 2 + c
    me_b = xh * 2 + b
    b_own, b_q, b_r, b_s = me_b, (1 - xh) * 2 + b, xh * 2 + (1 - b), (1 - xh) * 2 + (1 - b)
    dev = {
        "+": device((z + 1) % 8, x, y, c),
        "-": device((z + 7) % 8, x, y, c),
        "a": device(z, x, 3 - y, c),
        "b": device(z, x, y_of(a, 1 - b), c),
        "d": device(z, x, y, 1 - c),
        "xh": device(z, 3 - x, y, c),
        "xl": device(z, xh * 2 + (1 - rep), y, c),
        "c1": device(z, (1 - xh) * 2 + rep, y, c),
        "c3": device(z, (1 - xh) * 2 + rep, y_of(a, 1 - b), c),
    }

    def row_device(k, da, dc):
        off = ((k + 1) // 2) * (1 - 2 * (k % 2))
        zk, ak, ck = (z + off + 8) % 8, (a + da) % 2, (c + dc) % 2
        return zk, ak, ck, device(zk, x, y_of(ak, b), ck)

    barrier = pltpu.get_barrier_semaphore()

    def greet(t, _):
        pl.semaphore_signal(
            barrier, inc=1, device_id=row_device(t // 4, (t // 2) % 2, t % 2)[3], device_id_type=MESH
        )
        return 0

    lax.fori_loop(1, 32, greet, 0)
    for name in ("b", "c1", "c3", "xh", "xl"):
        pl.semaphore_signal(barrier, inc=1, device_id=dev[name], device_id_type=MESH)

    loads = [
        pltpu.make_async_copy(src, dst, local_sem.at[i])
        for i, (src, dst) in enumerate((
            (q_hbm, qbuf.at[me_q]),
            (db_hbm, dbraw.at[pl.ds(me_b * 4, 4)]),
            (three_hbm, three_v),
            (two_hbm, two_v),
            (one_hbm, one_v),
            (shard_hbm, shard_v),
            (local_hbm, local_v),
            (out_hbm, out_v),
        ))
    ]
    for load in loads:
        load.start()

    row8 = iota((8, 128), 0)
    for h in range(2):
        lens[me_b, pl.ds(h * 8, 8), :] = jnp.where(
            row8 % 2 == 0, frames[h * 2].astype(F32), frames[h * 2 + 1].astype(F32)
        )

    ids, started = {}, []

    def copy(name, src, dst, target):
        sem = ids.setdefault(name, len(ids))
        return pltpu.make_async_remote_copy(
            src_ref=src, dst_ref=dst, send_sem=send_sem.at[sem], recv_sem=recv_sem.at[sem],
            device_id=target, device_id_type=MESH,
        )

    def send(name, src, dst, target):
        started.append(copy(name, src, dst, target))
        started[-1].start()

    def wait(name, dst):
        copy(name, dst, dst, dev["d"]).wait_recv()

    def z_at(k):
        return (z + ((k + 1) // 2) * (1 - 2 * (k % 2)) + 8) % 8

    def half(zz, aa, h):
        return qbuf.at[zz * 4 + aa * 2 + c, pl.ds(h * 64, 64), :]

    def unit(zz, aa, cc):
        return qbuf.at[zz * 4 + aa * 2 + cc]

    def db_unit(block, u):
        return dbraw.at[block * 4 + u]

    pl.semaphore_wait(barrier, 36)

    def ring_send(way, d, item):
        k = 2 * (d - 1) - (1 if way == "+" else 0) if d > 1 else 0
        zz = z_at(k)
        ref = half(zz, 1 - a, 0) if item == 2 else half(zz, a, item)
        src = q_hbm.at[pl.ds(item * 64, 64), :] if d == 1 and item < 2 else ref
        send((way, d, item), src, ref, dev[way])

    def ring_wait(way, d, item):
        zz = z_at(2 * d - (1 if way == "+" else 0))
        wait((way, d, item), half(zz, 1 - a, 0) if item == 2 else half(zz, a, item))

    for h in range(2):
        ring_send("+", 1, h)
        ring_send("-", 1, h)
        send(("a", 0, h), q_hbm.at[pl.ds(h * 64, 64), :], half(z, a, h), dev["a"])

    def db_send(link, position):
        u = (2 * (1 - ell) + 1 + (3 * (position % 2)) + 2 * (position // 2)) % 4 if link == "xh" else (
            2 * (1 - ell) + position) % 4
        send((link, position), db_hbm.at[u], db_unit(me_b, u), dev[link])

    def db_wait(link, position):
        u = (2 * ell + 1 + (3 * (position % 2)) + 2 * (position // 2)) % 4 if link == "xh" else (
            2 * (1 - ell) + position) % 4
        wait((link, position), db_unit(b_q if link == "xh" else b_r, u))

    for position in range(2):
        db_send("xh", position)
        db_send("b", position)
    send(("d", 0, 0), q_hbm, unit(z, a, c), dev["d"])
    for name in ("b", "c1", "c3"):
        send(("len", name), lens.at[me_b], lens.at[me_b], dev[name])

    ri, ci = iota((256, 256), 0), iota((256, 256), 1)
    perm[...] = jnp.where(
        ci == (ri % 2) * 128 + ((ri // 2) % 8) * 16 + ri // 16, 1.0, 0.0
    ).astype(BF16)
    ri, ci = iota((256, 128), 0), iota((256, 128), 1)
    fold[...] = jnp.where((ri % 128) // 16 == ci // 16, 1.0 / 16.0, 0.0).astype(BF16)

    def permute(block, h):
        raw = dbraw[pl.ds(block * 4 + h * 2, 2)].reshape(256, K)
        dbp[block * 2 + h] = dot(perm[...], raw).astype(BF16)

    hbs = [
        b_own * 2, b_own * 2 + 1, b_q * 2 + ell, b_r * 2 + (1 - ell), b_s * 2 + ell,
        b_q * 2 + (1 - ell), b_r * 2 + ell, b_s * 2 + (1 - ell),
    ]

    def hb_at(o):
        total = jnp.int32(0)
        for i, value in enumerate(hbs):
            total = total + jnp.where(o == i, value, 0)
        return total

    def tile(hb, zz):
        left = dbp[hb]
        for n in range(2):
            right = qbuf[pl.ds(zz * 4 + n * 2, 2)].reshape(256, K)
            sim = lax.dot_general(left, right, (((1,), (1,)), ((), ())), preferred_element_type=F32)
            top = sim[0:16]
            for u in range(1, 16):
                top = jnp.maximum(top, sim[u * 16:(u + 1) * 16])
            for i in range(2):
                fmap[zz * 4 + n * 2 + i, hb] = top[:, i * 128:(i + 1) * 128]

    def tiles(os, ks):
        no, nk = len(os), len(ks)

        def body(t, _):
            tile(hb_at(os[0] + t % no), z_at(ks[0] + t // no))
            return 0

        lax.fori_loop(0, no * nk, body, 0)

    lane = iota((8, 128), 1)
    lane16 = lane % 16

    def post(k, first):
        zz = z_at(k)
        big = fmap[pl.ds(zz * 4, 4)].reshape(512, 128)
        maps = dot(jnp.concatenate(halves(big), axis=1), fold[...]) * (K ** -0.5)
        rows = jnp.zeros((8, 128), F32)
        for i in range(4):
            message = jnp.zeros((8, 128), F32)
            summit = jnp.zeros((8, 128), F32)
            for hb in range(8):
                length = lens[hb // 2, pl.ds((hb % 2) * 8, 8), :]
                parts = []
                for gh in range(2):
                    at = i * 128 + hb * 16 + gh * 8
                    present = (gh * 4 + row8 // 2).astype(F32) < length
                    parts.append(jnp.where(present, maps[at:at + 8], ABSENT))
                    message = jnp.where(lane16 == hb * 2 + gh, parts[-1], message)
                summit = jnp.where(lane16 // 2 == hb, jnp.maximum(*parts), summit)
            msg[zz * 4 + i] = message
            summit = jnp.maximum(summit, pltpu.roll(summit, 4, 0))
            summit = jnp.maximum(summit, pltpu.roll(summit, 2, 0))
            summit = jnp.where((row8 == lane % 2) & (row8 < 2), summit, 0.0)
            rows = jnp.where(row8 == i, jnp.sum(summit, axis=0, keepdims=True), rows)
        cbuf[me_b, zz] = rows
        for da in range(2):
            for dc in range(2):
                zk, ak, ck, target = row_device(k, da, dc)
                slot = zk * 4 + ak * 2 + ck
                if first and da == 0 and dc == 0:
                    rbuf[me_q] = msg[slot]
                else:
                    sem = k * 4 + da * 2 + dc
                    pltpu.make_async_remote_copy(
                        src_ref=msg.at[slot], dst_ref=rbuf.at[me_q], send_sem=msg_send.at[sem],
                        recv_sem=msg_recv.at[sem], device_id=target, device_id_type=MESH,
                    ).start()

    def weights_three():
        loads[2].wait()
        zero = jnp.zeros((64, 128), F32)
        for i in range(3):
            w = [three_v[(i * 3 + j) * 64:(i * 3 + j + 1) * 64, :] for j in range(3)]
            for r, (left, right) in enumerate(((w[1], w[0]), (w[2], w[1]), (zero, w[2]), (w[0], zero))):
                for s, part in enumerate((left, right)):
                    high, low = halves(part)
                    w3h[i, r * 64:(r + 1) * 64, s * 128:(s + 1) * 128] = high
                    w3l[i, r * 64:(r + 1) * 64, s * 128:(s + 1) * 128] = low

    def weights_rest():
        loads[3].wait()
        loads[4].wait()
        place = [jnp.where(iota((64, 128), 1) == iota((64, 128), 0) + 64 * s, 1.0, 0.0).astype(BF16) for s in range(2)]
        zero = jnp.zeros((32, 64), F32)
        for i in range(3):
            w = [two_v[(i * 3 + j) * 32:(i * 3 + j + 1) * 32, :] for j in range(3)]
            stacks = (jnp.concatenate(w + [zero], axis=0), jnp.concatenate([zero] + w, axis=0))
            for part in range(2):
                value = sum(dot(halves(stack)[part], where) for stack, where in zip(stacks, place)).astype(BF16)
                for r in range(2):
                    w2[i, r * 128:(r + 1) * 128, part * 128:(part + 1) * 128] = value
        spread = jnp.where(iota((32, 512), 1) % 32 == iota((32, 512), 0), 1.0, 0.0).astype(BF16)
        w1[...] = jnp.zeros((256, 512), BF16)
        j, col = iota((16, 512), 0), iota((16, 512), 1)
        g = (j % 2) * 4 + (j % 8) // 2
        pos = 2 * (col // 128) - 1 + (col % 128) // 32
        for part in range(2):
            for i in range(3):
                value = jnp.zeros((16, 512), F32)
                for s in range(3):
                    line = jnp.broadcast_to(one_v[i * 3 + s:i * 3 + s + 1, :], (16, 32))
                    line = dot(halves(line)[part], spread)
                    hit = (g - pos + 1 == s) & (pos >= 0) & (pos < 8)
                    value = value + jnp.where(hit, line, 0.0)
                w1[part * 128 + i * 16:part * 128 + (i + 1) * 16, :] = value.astype(BF16)

    def clear():
        none = jnp.zeros((128, 256), BF16)
        for p in range(4):
            x1[p, 0] = none
            x1[p, 9] = none
        for p in range(6):
            x2h[p, 0] = none
            x2h[p, 9] = none
            x2l[p, 0] = none
            x2l[p, 9] = none

        def edge(f, _):
            side = jnp.zeros((128, 128), BF16)
            x2h[1, f, :, 128:256] = side
            x2l[1, f, :, 128:256] = side
            x2h[4, f, :, 128:256] = side
            x2l[4, f, :, 128:256] = side
            return 0

        lax.fori_loop(1, 9, edge, 0)

    def share(way, d):
        k = 2 * d - (1 if way == "+" else 0)
        zz = z_at(k)
        send(("a", k, 1), half(zz, a, 1), half(zz, a, 1), dev["a"])
        send(("d", k, 0), unit(zz, a, c), unit(zz, a, c), dev["d"])

    def share_other(k):
        zz = z_at(k)
        send(("d", k, 1), unit(zz, 1 - a, c), unit(zz, 1 - a, c), dev["d"])

    def slab_wait(k):
        zz = z_at(k)
        wait(("d", k, 0), unit(zz, a, 1 - c))
        wait(("d", k, 1), unit(zz, 1 - a, 1 - c))

    def main_items(d):
        for item in range(2):
            for way in "+-":
                if d == 4 and way == "-":
                    continue
                ring_wait(way, d, item)
                if d < 3 or (d == 3 and way == "+"):
                    ring_send(way, d + 1, item)
        for way in "+-":
            if d < 4 or way == "+":
                share(way, d)

    def other_items(d):
        for way in "+-":
            if d == 4 and way == "+":
                continue
            ring_wait(way, d, 2)
            if d < 3 or (d == 3 and way == "-"):
                ring_send(way, d + 1, 2)
        for k in (2 * d - 1, 2 * d):
            if k < 8:
                wait(("a", k, 1), half(z_at(k), 1 - a, 1))
                share_other(k)

    loads[0].wait()
    wait(("a", 0, 0), half(z, 1 - a, 0))
    for way in "+-":
        ring_send(way, 1, 2)
    weights_three()
    wait(("a", 0, 1), half(z, 1 - a, 1))
    share_other(0)
    loads[1].wait()
    permute(b_own, 0)
    permute(b_own, 1)
    main_items(1)
    db_wait("xh", 0)
    send(("b", 4), db_unit(b_q, 2 * ell + 1), db_unit(b_q, 2 * ell + 1), dev["b"])
    db_wait("b", 0)
    send(("xh", 4), db_unit(b_r, 2 * (1 - ell)), db_unit(b_r, 2 * (1 - ell)), dev["xh"])
    for position in range(2, 4):
        db_send("xh", position)
        db_send("b", position)
    slab_wait(0)
    tiles((0, 1), (0,))
    weights_rest()
    other_items(1)
    clear()
    db_wait("xh", 1)
    db_wait("b", 1)
    permute(b_q, ell)
    permute(b_r, 1 - ell)
    slab_wait(1)
    slab_wait(2)
    tiles((0, 1, 2, 3), (1,))
    main_items(2)
    wait(("b", 4), db_unit(b_s, 2 * ell + 1))
    send(("xl", 1), db_unit(b_s, 2 * ell + 1), db_unit(b_s, 2 * ell + 1), dev["xl"])
    wait(("xh", 4), db_unit(b_s, 2 * ell))
    send(("xl", 0), db_unit(b_s, 2 * ell), db_unit(b_s, 2 * ell), dev["xl"])
    permute(b_s, ell)
    tiles((0, 1, 2, 3), (2,))
    other_items(2)
    tiles((2, 3), (0,))
    main_items(3)
    tiles((4,), (0, 1, 2))
    slab_wait(3)
    slab_wait(4)
    tiles((0, 1, 2, 3, 4), (3,))
    other_items(3)
    tiles((0, 1, 2, 3, 4), (4,))
    for position in range(2, 4):
        db_wait("xh", position)
        db_wait("b", position)
    permute(b_q, 1 - ell)
    permute(b_r, ell)
    main_items(4)
    tiles((5, 6), (0, 1, 2, 3, 4))
    other_items(4)
    for i in range(2):
        wait(("xl", i), db_unit(b_s, 2 * (1 - ell) + i))
    permute(b_s, 1 - ell)
    tiles((7,), (0, 1, 2, 3, 4))
    for name, block in (("b", b_r), ("c1", b_q), ("c3", b_s)):
        wait(("len", name), lens.at[block])
    post(0, True)

    def post_loop(k, _):
        post(k, False)
        return 0

    lax.fori_loop(1, 5, post_loop, 0)
    slab_wait(5)
    slab_wait(6)
    tiles((0, 1, 2, 3, 4, 5, 6, 7), (5, 6))
    slab_wait(7)
    tiles((0, 1, 2, 3, 4, 5, 6, 7), (7,))
    lax.fori_loop(5, 8, post_loop, 0)
    for name in ("b", "c1", "c3"):
        send(("coarse", name), cbuf.at[me_b], cbuf.at[me_b], dev[name])

    def column(row):
        return jnp.sum(
            jnp.where(iota((128, 128), 0) == iota((128, 128), 1), row.astype(F32), 0.0), axis=1, keepdims=True
        ).astype(jnp.int32)

    for i in (5, 6, 7):
        loads[i].wait()
    shard, place = column(shard_v[...]), column(local_v[...])
    cy = (shard // 2) % 4
    ca, cb = cy // 2, ((cy + 1) // 2) % 2
    source = (shard // 16) * 4 + ca * 2 + shard % 2
    chb = (((shard // 8) % 2) * 2 + cb) * 2 + place // 2
    base = source * 8 + place % 2
    cols = iota((128, 256), 1)
    onehot = jnp.concatenate(
        [jnp.where(cols == base + gl * 2, 1.0, 0.0).astype(BF16) for gl in range(4)], axis=0
    )

    def msg_copy(k, da, dc):
        off = ((k + 1) // 2) * (1 - 2 * (k % 2))
        slot = ((z - off + 8) % 8) * 4 + ((a + da) % 2) * 2 + (c + dc) % 2
        sem = k * 4 + da * 2 + dc
        return pltpu.make_async_remote_copy(
            src_ref=msg.at[slot], dst_ref=rbuf.at[slot], send_sem=msg_send.at[sem],
            recv_sem=msg_recv.at[sem], device_id=dev["d"], device_id_type=MESH,
        )

    def msg_wait(t, _):
        msg_copy(t // 4, (t // 2) % 2, t % 2).wait_recv()
        return 0

    lax.fori_loop(1, 32, msg_wait, 0)
    chosen = pick(onehot, rbuf[...].reshape(256, 128))
    lane = iota((128, 128), 1)
    lane16 = lane % 16
    maps = jnp.zeros((128, 128), F32)
    for gl in range(4):
        t = chosen[gl * 128:(gl + 1) * 128]
        for bit in (4, 2, 1):
            t = jnp.where((chb // bit) % 2 == 1, pltpu.roll(t, 128 - 2 * bit, 1), t)
        if gl:
            t = pltpu.roll(t, 2 * gl, 1)
        maps = jnp.where(lane16 // 2 == gl, t, maps)
    there = maps > ABSENT / 2
    for g in range(8):
        at = (g % 4) * 2 + g // 4
        pen[g] = jnp.where(there, 0.0, -3e38)[:, at:at + 1]
    maps = jnp.where(there & (lane16 < 8), maps, 0.0)
    high = maps.astype(BF16).astype(F32)
    both = jnp.where(lane16 < 8, high, pltpu.roll(maps - high, 8, 1))
    for f in range(8):
        around = pltpu.roll(both, (128 - 16 * (f - 1)) % 128, 1) if f != 1 else both
        if f == 0:
            around = jnp.where(lane < 16, 0.0, around)
        if f == 7:
            around = jnp.where(lane // 16 == 2, 0.0, around)
        around = around.astype(BF16)
        out = jnp.maximum(dot(jnp.concatenate([around, around], axis=1), w1[...]), 0.0)
        high1, low1 = halves(out)
        for p in range(4):
            x1[p, f + 1, :, 0:128] = high1[:, p * 128:(p + 1) * 128]
            x1[p, f + 1, :, 128:256] = low1[:, p * 128:(p + 1) * 128]

    def second(p, _):
        out = jnp.zeros((1024, 256), F32)
        for i in range(3):
            out = out + dot(x1[p, i:i + 8].reshape(1024, 256), w2[i])
        out = jnp.maximum(out[:, :128] + out[:, 128:], 0.0)
        for ref, part in zip((x2h, x2l), halves(out)):
            part = part.reshape(8, 128, 128)
            ref[p + 1, 1:9, :, 0:128] = part
            ref[p, 1:9, :, 128:192] = part[:, :, 0:64]
            ref[p + 2, 1:9, :, 192:256] = part[:, :, 64:128]
        return 0

    lax.fori_loop(0, 4, second, 0)
    scale = jnp.concatenate([out_v[...], out_v[...]], axis=1)
    best[...] = jnp.full((1024, 1), -3e38, F32)

    def third(p, _):
        out = jnp.zeros((1024, 256), F32)
        for i in range(3):
            upper = x2h[p + 1, i:i + 8].reshape(1024, 256)
            lower = x2l[p + 1, i:i + 8].reshape(1024, 256)
            out = out + dot(upper, w3h[i]) + dot(lower, w3h[i]) + dot(upper, w3l[i])
        out = jnp.maximum(out, 0.0) * scale
        for s in range(2):
            total = jnp.sum(out[:, s * 128:(s + 1) * 128], axis=1, keepdims=True)
            total = total.reshape(8, 128, 1) + pen[2 * p + s][None]
            best[...] = jnp.maximum(best[...], total.reshape(1024, 1))
        return 0

    lax.fori_loop(0, 4, third, 0)
    mean = jnp.sum(best[...].reshape(8, 128, 1), axis=0) * 0.125
    refined_ref[...] = jnp.sum(
        jnp.where(iota((128, 128), 0) == iota((128, 128), 1), mean, 0.0), axis=0, keepdims=True
    )

    for name, block in (("b", b_r), ("c1", b_q), ("c3", b_s)):
        wait(("coarse", name), cbuf.at[block])
    n, col = iota((128, 256), 0), iota((128, 256), 1)
    ny = (n // 2) % 4
    want = (((n // 8) % 2) * 2 + ((ny + 1) // 2) % 2) * 64 + (n // 16) * 8 + (ny // 2) * 2 + n % 2
    scores = pick(jnp.where(col == want, 1.0, 0.0).astype(BF16), cbuf[...].reshape(256, 128))
    for shift in (64, 32, 16):
        scores = scores + pltpu.roll(scores, shift, 1)
    scores = scores * 0.125
    mine = scores
    for block in range(1, 4):
        mine = jnp.where(me_b == block, pltpu.roll(scores, 128 - 4 * block, 1), mine)
    coarse_ref[...] = mine[:, 0:4]

    for sent in started:
        sent.wait_send()

    def sent_wait(t, _):
        msg_copy(t // 4, (t // 2) % 2, t % 2).wait_send()
        return 0

    lax.fori_loop(1, 32, sent_wait, 0)


def local(queries, database, db_frames, cand_shard, cand_local, conv_one, conv_two, conv_three, conv_out):
    anywhere = pl.BlockSpec(memory_space=pl.ANY)
    vmem = pl.BlockSpec(memory_space=pltpu.VMEM)
    smem = pl.BlockSpec(memory_space=pltpu.SMEM)
    coarse, refined = pl.pallas_call(
        kernel,
        out_shape=(jax.ShapeDtypeStruct((128, 4), F32), jax.ShapeDtypeStruct((1, 128), F32)),
        in_specs=[anywhere, anywhere, smem] + [anywhere] * 6,
        out_specs=(vmem, vmem),
        scratch_shapes=[
            pltpu.VMEM((32, 128, K), BF16),
            pltpu.VMEM((16, 128, K), BF16),
            pltpu.VMEM((8, 256, K), BF16),
            pltpu.VMEM((32, 8, 16, 128), F32),
            pltpu.VMEM((4, 16, 128), F32),
            pltpu.VMEM((32, 8, 128), F32),
            pltpu.VMEM((32, 8, 128), F32),
            pltpu.VMEM((4, 8, 8, 128), F32),
            pltpu.VMEM((256, 256), BF16),
            pltpu.VMEM((256, 128), BF16),
            pltpu.VMEM((1, 128), jnp.int32),
            pltpu.VMEM((1, 128), jnp.int32),
            pltpu.VMEM((9, 32), F32),
            pltpu.VMEM((288, 64), F32),
            pltpu.VMEM((576, 128), F32),
            pltpu.VMEM((1, 128), F32),
            pltpu.VMEM((256, 512), BF16),
            pltpu.VMEM((3, 256, 256), BF16),
            pltpu.VMEM((3, 256, 256), BF16),
            pltpu.VMEM((3, 256, 256), BF16),
            pltpu.VMEM((4, 10, 128, 256), BF16),
            pltpu.VMEM((6, 10, 128, 256), BF16),
            pltpu.VMEM((6, 10, 128, 256), BF16),
            pltpu.VMEM((8, 128, 1), F32),
            pltpu.VMEM((1024, 1), F32),
            pltpu.SemaphoreType.DMA((72,)),
            pltpu.SemaphoreType.DMA((72,)),
            pltpu.SemaphoreType.DMA((32,)),
            pltpu.SemaphoreType.DMA((32,)),
            pltpu.SemaphoreType.DMA((8,)),
        ],
        compiler_params=pltpu.CompilerParams(
            collective_id=0, has_side_effects=True, vmem_limit_bytes=52 * 1024 * 1024
        ),
        cost_estimate=pl.CostEstimate(flops=13_000_000_000, bytes_accessed=2_000_000, transcendentals=0),
    )(
        queries.reshape(128, K), database.reshape(4, 128, K), db_frames, cand_shard.reshape(1, 128),
        cand_local.reshape(1, 128), conv_one.reshape(9, 32), conv_two.reshape(288, 64),
        conv_three.reshape(576, 128), conv_out.reshape(1, 128),
    )
    return coarse[None], refined[None]


def solution(mesh):
    in_specs = (
        P("index", "rep", None, None, None),
        P("index", None, None, None),
        P("index"),
        P("index", "rep", None, None),
        P("index", "rep", None),
        P(),
        P(),
        P(),
        P(),
    )
    out_specs = (P("rep", None, "index"), P("index", "rep", None))
    return jax.shard_map(local, mesh=mesh, in_specs=in_specs, out_specs=out_specs, check_vma=False)
```

time: 494 us -> 81.8 us (0.17)
  waiting for transfers between devices: 146 us -> 0 us
  matrix products: 132 us -> 0 us
  local copies, waits for them, and re-layouts: 122 us -> 6.33 us
  Pallas kernels: 0 us -> 74.5 us
  other arithmetic: 52.4 us -> 0.03 us
  starting transfers between devices: 25.1 us -> 0 us
  between operations: 14.5 us -> 0.69 us
    all_gather x1 -> x0, waiting for transfers between devices: 124 us -> none  [local(): piece = lax.all_gather(queries[:, 0], 'index', axis=0, tiled=True)]
    conv_general_dilated x3 -> x0, matrix products: 89 us -> none  [convolve(): lax.conv_general_dilated(inputs, kernel, (1, 1), 'SAME', dimension_number...]
    pallas_call x0 -> x1, Pallas kernels: none -> 74.5 us  [local(): pl.pallas_call(kernel, out_shape=(jax.ShapeDtypeStruct((128, 4), F32), ja...]
    reduce_max x18 -> x0, other arithmetic: 43.9 us -> none  [the longest x16 41.5 us: block_frame_maps(): region_best = jnp.max(similar, axis=2)]
    dot_general x18 -> x0, matrix products: 43.1 us -> none  [the longest x16 33.5 us: block_frame_maps(): jnp.dot(clip_rows, query_cols.T, preferred_element_type=jnp.float32)]
    reshape x18 -> x1, local copies, waits for them, and re-layouts: 40.4 us -> 0.01 us  [local(): conv_one.reshape(9, 32)]
    dynamic_slice x32 -> x0, local copies, waits for them, and re-layouts: 31.4 us -> none  [local(): all_maps = lax.map(lambda block: block_frame_maps(block, database), grouped)]
    mul x16 -> x0, local copies, waits for them, and re-layouts: 30.7 us -> none  [block_frame_maps(): jnp.dot(clip_rows, query_cols.T, preferred_element_type=jnp.float32)]
  transfers between devices with their start and end apart: 3 -> 0, of which waited for: 3 -> 0; matrix products, arithmetic and copies ran while one was open for 2% -> 0% of each run, Pallas kernels for 0% -> 0%
where the time goes in v1:
time: 81.8 us; the launch traced here: 81.6 us
  Pallas kernels  74.5 us (91%)
  local copies, waits for them, and re-layouts  6.33 us (8%)
    pallas_call x1, Pallas kernels, local(): pl.pallas_call(kernel, out_shape=(jax.ShapeDtypeStruct((128, 4), F32), ja...  74.5 us
    unnamed x20, local copies, waits for them, and re-layouts  6.32 us

profile of v1, /device:TPU:1, one launch (start us, length us, event | category | flops | bytes accessed | tf_op | source)
XLA Modules:
  0.0 81.6 jit_solution(8756085012326008609)
XLA Ops:
  0.6 0.0 copy-start.8
  0.6 0.7 copy-done.8
  1.3 0.0 copy-start.4
  1.4 0.0 copy-start.5
  1.4 0.0 copy-start.6
  1.4 0.0 copy-start.7
  1.4 0.6 copy-done.4
  2.0 0.0 copy-done.5
  2.0 0.0 copy-done.6
  2.0 0.0 copy-done.7
  2.1 0.0 copy-start
  2.1 1.0 %copy-done = bf16[4,8,16,512]{3,2,1,0:T(8,128)(2,1)S(1)} copy-done((bf16[4,8,16,512]{3,2,1,0:T(8,128)(2,1)S(1)}, bf16[4,8,16,512]{3,2,1,0:T(8,128)(2,1)}, u32[]{:S(2)}) %copy-start) | copy-done | bytes 524312
  3.1 0.0 copy-start.1
  3.1 1.0 %copy-done.1 = f32[3,3,64,128]{3,2,1,0:T(8,128)S(1)} copy-done((f32[3,3,64,128]{3,2,1,0:T(8,128)S(1)}, f32[3,3,64,128]{3,2,1,0:T(8,128)}, u32[]{:S(2)}) %copy-start.1) | copy-done | bytes 294936
  4.1 0.0 copy-start.2
  4.1 0.9 %copy-done.2 = f32[3,3,32,64]{3,2,1,0:T(8,128)S(1)} copy-done((f32[3,3,32,64]{3,2,1,0:T(8,128)S(1)}, f32[3,3,32,64]{3,2,1,0:T(8,128)}, u32[]{:S(2)}) %copy-start.2) | copy-done | bytes 73752
  5.0 0.0 copy-start.3
  5.0 0.9 %copy-done.3 = bf16[1,1,8,16,512]{4,3,2,1,0:T(8,128)(2,1)S(1)} copy-done((bf16[1,1,8,16,512]{4,3,2,1,0:T(8,128)(2,1)S(1)}, bf16[1,1,8,16,512]{4,3,2,1,0:T(8,128)(2,1)}, u32[]{:S(2)}) %copy-start.3) | copy-done | bytes 131096
  5.9 74.5 %shard_map.104 = (f32[128,4]{1,0:T(8,128)S(1)}, f32[1,128]{1,0:T(1,128)S(1)}) custom-call(bf16[128,512]{1,0:T(8,128)(2,1)S(1)} %bitcast.13, bf16[4,128,512]{2,1,0:T(8,128)(2,1)S(1)} %bitcast.10, s32[4]{0:T(128)S(1)} %copy-done.4, s32[1,128]{1,0:T(1,128)S(1)} %bitcast.14, s32[1,128]{1,0:T(1,128)S(1)} %bitcast.15, f32[9,32]{1,0:T(8,128)S(1)} %reshape.32.one_hbm, ...), custom_call_target="tpu_custom_call" | custom-call | flops 12999999488 | bytes 2000000 | tf_op jit(solution)/shard_map/pallas_call | solution.py:560
  80.4 0.7 copy.11
  81.0 0.5 copy.14
  (2 shorter events, 0.0 us)
Async XLA Ops:
  0.6 0.7 copy-start.8
  1.3 0.7 copy-start.4
  1.4 0.7 copy-start.5
  1.4 0.7 copy-start.6
  1.4 0.7 copy-start.7
  2.1 1.0 %copy-start = (bf16[4,8,16,512]{3,2,1,0:T(8,128)(2,1)S(1)}, bf16[4,8,16,512]{3,2,1,0:T(8,128)(2,1)}, u32[]{:S(2)}) copy-start(bf16[4,8,16,512]{3,2,1,0:T(8,128)(2,1)} %param.10) | copy-start | bytes 1572868
  3.1 1.0 %copy-start.1 = (f32[3,3,64,128]{3,2,1,0:T(8,128)S(1)}, f32[3,3,64,128]{3,2,1,0:T(8,128)}, u32[]{:S(2)}) copy-start(f32[3,3,64,128]{3,2,1,0:T(8,128)} %param.16) | copy-start | bytes 884740
  4.1 0.9 %copy-start.2 = (f32[3,3,32,64]{3,2,1,0:T(8,128)S(1)}, f32[3,3,32,64]{3,2,1,0:T(8,128)}, u32[]{:S(2)}) copy-start(f32[3,3,32,64]{3,2,1,0:T(8,128)} %param.15) | copy-start | bytes 221188
  5.0 0.9 %copy-start.3 = (bf16[1,1,8,16,512]{4,3,2,1,0:T(8,128)(2,1)S(1)}, bf16[1,1,8,16,512]{4,3,2,1,0:T(8,128)(2,1)}, u32[]{:S(2)}) copy-start(bf16[1,1,8,16,512]{4,3,2,1,0:T(8,128)(2,1)} %param.9) | copy-start | bytes 393220

commit v2 on v1

v2 whole, which is shorter than its diff:
```python
import functools

import jax
import jax.numpy as jnp
from jax import lax
from jax.experimental import pallas as pl
from jax.experimental.pallas import tpu as pltpu
from jax.sharding import PartitionSpec as P

MESH = pl.DeviceIdType.MESH
F32, BF16 = jnp.float32, jnp.bfloat16
ABSENT = -(2.0 ** 100)
K = 512


def dot(a, b):
    return jnp.dot(a, b, preferred_element_type=F32)


def iota(shape, axis):
    return lax.broadcasted_iota(jnp.int32, shape, axis)


def halves(x):
    high = x.astype(BF16)
    return high, (x - high.astype(F32)).astype(BF16)


def thirds(x):
    high, rest = x.astype(BF16), None
    rest = x - high.astype(F32)
    mid = rest.astype(BF16)
    return high, mid, (rest - mid.astype(F32)).astype(BF16)


def pick(onehot, x):
    y = dot(onehot, jnp.concatenate(thirds(x), axis=1))
    n = x.shape[1]
    return y[:, :n] + (y[:, n:2 * n] + y[:, 2 * n:])


def kernel(
    q_hbm, db_hbm, frames, shard_hbm, local_hbm, one_hbm, two_hbm, three_hbm, out_hbm,
    coarse_ref, refined_ref,
    qbuf, dbraw, dba, dbb, fmap, lens, msg, rbuf, cbuf, perm,
    shard_v, local_v, one_v, two_v, three_v, out_v,
    w1, w2, w3, x1, x2h, x2l, pen, best,
    send_sem, recv_sem, msg_send, msg_recv, local_sem,
):
    index, rep = lax.axis_index("index"), lax.axis_index("rep")
    c, y, xh, z = index % 2, (index // 2) % 4, (index // 8) % 2, index // 16
    x = xh * 2 + rep
    a, b = y // 2, ((y + 1) // 2) % 2
    ell = rep

    def device(z, x, y, c):
        return (((z * 2 + x // 2) * 4 + y) * 2 + c, x % 2)

    def y_of(a, b):
        return a * 3 + b * (1 - 2 * a)

    me_q = z * 4 + a * 2 + c
    me_b = xh * 2 + b
    b_own, b_q, b_r, b_s = me_b, (1 - xh) * 2 + b, xh * 2 + (1 - b), (1 - xh) * 2 + (1 - b)
    dev = {
        "+": device((z + 1) % 8, x, y, c),
        "-": device((z + 7) % 8, x, y, c),
        "a": device(z, x, 3 - y, c),
        "b": device(z, x, y_of(a, 1 - b), c),
        "d": device(z, x, y, 1 - c),
        "xh": device(z, 3 - x, y, c),
        "xl": device(z, xh * 2 + (1 - rep), y, c),
        "c1": device(z, (1 - xh) * 2 + rep, y, c),
        "c3": device(z, (1 - xh) * 2 + rep, y_of(a, 1 - b), c),
    }

    def row_device(k, da, dc):
        off = ((k + 1) // 2) * (1 - 2 * (k % 2))
        zk, ak, ck = (z + off + 8) % 8, (a + da) % 2, (c + dc) % 2
        return zk, ak, ck, device(zk, x, y_of(ak, b), ck)

    barrier = pltpu.get_barrier_semaphore()
    for target in dev.values():
        pl.semaphore_signal(barrier, inc=1, device_id=target, device_id_type=MESH)

    loads = [
        pltpu.make_async_copy(src, dst, local_sem.at[i])
        for i, (src, dst) in enumerate((
            (q_hbm, qbuf.at[me_q]),
            (db_hbm, dbraw.at[pl.ds(me_b * 4, 4)]),
            (three_hbm, three_v),
            (two_hbm, two_v),
            (one_hbm, one_v),
            (shard_hbm, shard_v),
            (local_hbm, local_v),
            (out_hbm, out_v),
        ))
    ]
    for load in loads:
        load.start()

    row8 = iota((8, 128), 0)
    own_lens = jnp.zeros((8, 128), F32)
    for u in range(4):
        own_lens = jnp.where(row8 == u, frames[u].astype(F32), own_lens)
    lens[me_b] = own_lens

    ids, started = {}, []

    def copy(name, src, dst, target):
        sem = ids.setdefault(name, len(ids))
        return pltpu.make_async_remote_copy(
            src_ref=src, dst_ref=dst, send_sem=send_sem.at[sem], recv_sem=recv_sem.at[sem],
            device_id=target, device_id_type=MESH,
        )

    def send(name, src, dst, target):
        started.append(copy(name, src, dst, target))
        started[-1].start()

    def wait(name, dst):
        copy(name, dst, dst, dev["d"]).wait_recv()

    def z_at(k):
        return (z + ((k + 1) // 2) * (1 - 2 * (k % 2)) + 8) % 8

    def half(zz, aa, h):
        return qbuf.at[zz * 4 + aa * 2 + c, pl.ds(h * 64, 64), :]

    def unit(zz, aa, cc):
        return qbuf.at[zz * 4 + aa * 2 + cc]

    def db_unit(block, u):
        return dbraw.at[block * 4 + u]

    pl.semaphore_wait(barrier, len(dev))

    def ring_send(way, d, item):
        k = 2 * (d - 1) - (1 if way == "+" else 0) if d > 1 else 0
        zz = z_at(k)
        ref = half(zz, 1 - a, 0) if item == 2 else half(zz, a, item)
        src = q_hbm.at[pl.ds(item * 64, 64), :] if d == 1 and item < 2 else ref
        send((way, d, item), src, ref, dev[way])

    def ring_wait(way, d, item):
        zz = z_at(2 * d - (1 if way == "+" else 0))
        wait((way, d, item), half(zz, 1 - a, 0) if item == 2 else half(zz, a, item))

    for h in range(2):
        ring_send("+", 1, 1 - h)
        ring_send("-", 1, 1 - h)
        send(("a", 0, h), q_hbm.at[pl.ds(h * 64, 64), :], half(z, a, h), dev["a"])

    def db_send(link, position):
        u = (2 * (1 - ell) + 1 + (3 * (position % 2)) + 2 * (position // 2)) % 4 if link == "xh" else (
            2 * (1 - ell) + position) % 4
        send((link, position), db_hbm.at[u], db_unit(me_b, u), dev[link])

    def db_wait(link, position):
        u = (2 * ell + 1 + (3 * (position % 2)) + 2 * (position // 2)) % 4 if link == "xh" else (
            2 * (1 - ell) + position) % 4
        wait((link, position), db_unit(b_q if link == "xh" else b_r, u))

    for position in range(2):
        db_send("xh", position)
        db_send("b", position)
    send(("d", 0, 0), q_hbm, unit(z, a, c), dev["d"])
    for name in ("b", "c1", "c3"):
        send(("len", name), lens.at[me_b], lens.at[me_b], dev[name])

    ri, ci = iota((256, 256), 0), iota((256, 256), 1)
    perm[...] = jnp.where(
        ci == (ri % 2) * 128 + ((ri // 2) % 8) * 16 + ri // 16, 1.0, 0.0
    ).astype(BF16)

    def permute(hb, first, second):
        raw = jnp.concatenate([dbraw[first[0] * 4 + first[1]], dbraw[second[0] * 4 + second[1]]], axis=0)
        rows = dot(perm[...], raw).astype(BF16)
        for u in range(16):
            piece = rows[u * 16:(u + 1) * 16]
            if hb < 4:
                at = (u % 4) * 64 + hb * 16
                dba[u // 4, at:at + 16, :] = piece
            else:
                at = (u % 8) * 32 + (hb % 2) * 16
                dbb[hb // 2 - 2, u // 8, at:at + 16, :] = piece

    lane = iota((8, 128), 1)

    def tile(group, k):
        zz = z_at(k)
        left = qbuf[pl.ds(zz * 4, 4)].reshape(512, K)
        top = None
        for t in range(4 if group == 0 else 2):
            right = dba[t] if group == 0 else dbb[group - 1, t]
            sim = lax.dot_general(left, right, (((1,), (1,)), ((), ())), preferred_element_type=F32)
            sim = jnp.maximum(sim[:, :128], sim[:, 128:])
            top = sim if top is None else jnp.maximum(top, sim)
        top = jnp.maximum(top, pltpu.roll(top, 64, 1))
        if group:
            top = jnp.maximum(top, pltpu.roll(top, 32, 1))
        mean = jnp.sum(top.reshape(32, 16, 128), axis=1).reshape(4, 8, 128)
        at = pl.ds(zz * 4, 4)
        if group:
            mean = jnp.where((lane // 32 == group + 1)[None], mean, fmap[at])
        fmap[at] = mean

    order = {
        "own": ((0, 0), (0, 1), (1, 0), (1, 1)),
        "q": ((3, 0), (2, 0), (6, 0), (5, 0)),
        "r": ((5, 1), (6, 1), (2, 1), (3, 1)),
        "s": ((4, 0), (4, 1), (7, 0), (7, 1)),
    }
    blocks = {"own": b_own, "q": b_q, "r": b_r, "s": b_s}

    def unit_of(name, i):
        return i if name == "own" else (2 * ell + i) % 4

    def length_lanes():
        total = jnp.zeros((1, 128), F32)
        lane1 = iota((1, 128), 1)
        for name, places in order.items():
            for i, (hb, v) in enumerate(places):
                value = lens[blocks[name], pl.ds(unit_of(name, i), 1), :]
                total = jnp.where((lane1 // 16 == hb) & (lane1 % 2 == v), value, total)
        return (lane1 % 16 // 2).astype(F32) < total

    def post(k, first):
        zz = z_at(k)
        rows = jnp.zeros((8, 128), F32)
        for i in range(4):
            maps = fmap[zz * 4 + i] * (K ** -0.5 / 16)
            maps = jnp.where(present, maps, ABSENT)
            msg[zz * 4 + i] = maps
            for shift in (8, 4, 2):
                maps = jnp.maximum(maps, pltpu.roll(maps, 128 - shift, 1))
            rows = jnp.where(row8 == i, jnp.sum(maps, axis=0, keepdims=True), rows)
        cbuf[me_b, zz] = rows
        for da in range(2):
            for dc in range(2):
                zk, ak, ck, target = row_device(k, da, dc)
                slot = zk * 4 + ak * 2 + ck
                if first and da == 0 and dc == 0:
                    rbuf[me_q] = msg[slot]
                else:
                    sem = k * 4 + da * 2 + dc
                    pltpu.make_async_remote_copy(
                        src_ref=msg.at[slot], dst_ref=rbuf.at[me_q], send_sem=msg_send.at[sem],
                        recv_sem=msg_recv.at[sem], device_id=target, device_id_type=MESH,
                    ).start()

    def weights_three():
        loads[2].wait()
        zero = jnp.zeros((64, 128), F32)
        for i in range(3):
            w = [three_v[(i * 3 + j) * 64:(i * 3 + j + 1) * 64, :] for j in range(3)]
            for r, (left, right) in enumerate(((w[1], w[0]), (w[2], w[1]), (zero, w[2]), (w[0], zero))):
                for s, part in enumerate((left, right)):
                    high, low = halves(part)
                    for at, value in ((0, high), (256, high), (512, low)):
                        at = i * 768 + at + r * 64
                        w3[at:at + 64, s * 128:(s + 1) * 128] = value

    def weights_rest():
        loads[3].wait()
        loads[4].wait()
        place = [jnp.where(iota((64, 128), 1) == iota((64, 128), 0) + 64 * s, 1.0, 0.0).astype(BF16) for s in range(2)]
        zero = jnp.zeros((32, 64), F32)
        for i in range(3):
            w = [two_v[(i * 3 + j) * 32:(i * 3 + j + 1) * 32, :] for j in range(3)]
            stacks = (jnp.concatenate(w + [zero], axis=0), jnp.concatenate([zero] + w, axis=0))
            for part in range(2):
                value = sum(dot(halves(stack)[part], where) for stack, where in zip(stacks, place)).astype(BF16)
                for r in range(2):
                    w2[i * 256 + r * 128:i * 256 + (r + 1) * 128, part * 128:(part + 1) * 128] = value
        spread = jnp.where(iota((32, 512), 1) % 32 == iota((32, 512), 0), 1.0, 0.0).astype(BF16)
        w1[...] = jnp.zeros((256, 512), BF16)
        j, col = iota((32, 512), 0), iota((32, 512), 1)
        g = (j % 16) // 2
        pos = 2 * (col // 128) - 1 + (col % 128) // 32
        for part in range(2):
            for i in range(3):
                value = jnp.zeros((32, 512), F32)
                for s in range(3):
                    line = dot(halves(jnp.broadcast_to(one_v[i, s], (16, 32)))[part], spread)[0:1]
                    hit = (g - pos + 1 == s) & (pos >= 0) & (pos < 8) & (j % 2 == 0)
                    value = value + jnp.where(hit, line, 0.0)
                w1[part * 128 + i * 32:part * 128 + (i + 1) * 32, :] = value.astype(BF16)

    def clear():
        none = jnp.zeros((128, 256), BF16)
        for p in range(4):
            x1[p, 0] = none
            x1[p, 9] = none
        for p in range(6):
            x2h[p, 0] = none
            x2h[p, 9] = none
            x2l[p, 0] = none
            x2l[p, 9] = none

        def edge(f, _):
            side = jnp.zeros((128, 128), BF16)
            x2h[1, f, :, 128:256] = side
            x2l[1, f, :, 128:256] = side
            x2h[4, f, :, 128:256] = side
            x2l[4, f, :, 128:256] = side
            return 0

        lax.fori_loop(1, 9, edge, 0)

    def share_other(k):
        zz = z_at(k)
        send(("d", k, 1), unit(zz, 1 - a, c), unit(zz, 1 - a, c), dev["d"])

    def slab_wait(k):
        zz = z_at(k)
        wait(("d", k, 0), unit(zz, a, 1 - c))
        wait(("d", k, 1), unit(zz, 1 - a, 1 - c))

    def main_item(d, item):
        for way in "+-" if d < 4 else "+":
            k = 2 * d - (1 if way == "+" else 0)
            zz = z_at(k)
            ring_wait(way, d, item)
            if d < 3 or (d == 3 and way == "+"):
                ring_send(way, d + 1, item)
            if item == 1:
                send(("a", k, 1), half(zz, a, 1), half(zz, a, 1), dev["a"])
            else:
                send(("d", k, 0), unit(zz, a, c), unit(zz, a, c), dev["d"])

    def other_item(d):
        for way in "+-" if d < 4 else "-":
            ring_wait(way, d, 2)
            if d < 3 or (d == 3 and way == "-"):
                ring_send(way, d + 1, 2)

    def partner_item(d):
        for k in (2 * d - 1, 2 * d) if d < 4 else (7,):
            wait(("a", k, 1), half(z_at(k), 1 - a, 1))
            share_other(k)

    q_units = [(b_q, (2 * ell + i) % 4) for i in (1, 0, 3, 2)]
    r_units = [(b_r, (2 * ell + i) % 4) for i in (2, 3, 0, 1)]
    s_units = [(b_s, (2 * ell + i) % 4) for i in range(4)]

    loads[0].wait()
    wait(("a", 0, 0), half(z, 1 - a, 0))
    for way in "+-":
        ring_send(way, 1, 2)
    loads[1].wait()
    permute(0, (b_own, 0), (b_own, 1))
    main_item(1, 1)
    permute(1, (b_own, 2), (b_own, 3))
    wait(("a", 0, 1), half(z, 1 - a, 1))
    share_other(0)
    main_item(1, 0)
    db_wait("xh", 0)
    send(("b", 4), db_unit(b_q, 2 * ell + 1), db_unit(b_q, 2 * ell + 1), dev["b"])
    db_wait("b", 0)
    send(("xh", 4), db_unit(b_r, 2 * (1 - ell)), db_unit(b_r, 2 * (1 - ell)), dev["xh"])
    db_send("xh", 2)
    db_send("b", 2)
    permute(2, q_units[0], r_units[0])
    other_item(1)
    weights_three()
    partner_item(1)
    db_wait("xh", 1)
    db_wait("b", 1)
    db_send("xh", 3)
    db_send("b", 3)
    permute(3, q_units[1], r_units[1])
    main_item(2, 1)
    slab_wait(0)
    tile(0, 0)
    main_item(2, 0)
    slab_wait(1)
    slab_wait(2)
    tile(0, 1)
    other_item(2)
    tile(0, 2)
    weights_rest()
    partner_item(2)
    wait(("b", 4), db_unit(b_s, 2 * ell + 1))
    wait(("xh", 4), db_unit(b_s, 2 * ell))
    for i in range(2):
        send(("xl", i), db_unit(b_s, 2 * ell + i), db_unit(b_s, 2 * ell + i), dev["xl"])
    permute(4, s_units[0], s_units[1])
    main_item(3, 1)
    clear()
    slab_wait(3)
    tile(0, 3)
    slab_wait(4)
    tile(0, 4)
    for name, block in (("b", b_r), ("c1", b_q), ("c3", b_s)):
        wait(("len", name), lens.at[block])
    present = length_lanes()
    main_item(3, 0)
    db_wait("xh", 2)
    db_wait("b", 2)
    permute(5, q_units[2], r_units[2])
    tile(1, 0)
    tile(1, 1)
    other_item(3)
    tile(1, 2)
    partner_item(3)
    tile(1, 3)
    tile(1, 4)
    slab_wait(5)
    tile(0, 5)
    main_item(4, 1)
    tile(1, 5)
    slab_wait(6)
    tile(0, 6)
    tile(1, 6)
    db_wait("xh", 3)
    db_wait("b", 3)
    permute(6, q_units[3], r_units[3])
    for i in range(2):
        wait(("xl", i), db_unit(b_s, 2 * (1 - ell) + i))
    permute(7, s_units[2], s_units[3])
    main_item(4, 0)
    tile(2, 0)
    tile(2, 1)
    other_item(4)
    partner_item(4)
    for k in range(2, 7):
        tile(2, k)
    slab_wait(7)
    tile(0, 7)
    tile(1, 7)
    tile(2, 7)
    post(0, True)

    def post_loop(k, _):
        post(k, False)
        return 0

    lax.fori_loop(1, 8, post_loop, 0)
    ri, ci = iota((128, 128), 0), iota((128, 128), 1)
    where = ri < 0
    for r, (name, places) in enumerate(order.items()):
        for i, (hb, v) in enumerate(places):
            where = where | ((ri == hb * 16 + v) & (ci == r * 32 + unit_of(name, i)))
    sums = cbuf[me_b].reshape(64, 128)
    where = jnp.where(where, 1.0, 0.0).astype(BF16)
    sums = sum(dot(part, where) for part in thirds(sums)) * 0.125
    cbuf[me_b] = sums.reshape(8, 8, 128)
    for name in ("b", "c1", "c3"):
        send(("coarse", name), cbuf.at[me_b], cbuf.at[me_b], dev[name])

    def column(row):
        return jnp.sum(
            jnp.where(iota((128, 128), 0) == iota((128, 128), 1), row.astype(F32), 0.0), axis=1, keepdims=True
        ).astype(jnp.int32)

    for i in (5, 6, 7):
        loads[i].wait()
    shard, place = column(shard_v[...]), column(local_v[...])
    cy = (shard // 2) % 4
    ca, cb = cy // 2, ((cy + 1) // 2) % 2
    source = (shard // 16) * 4 + ca * 2 + shard % 2
    cross, other = ((shard // 8) % 2) != xh, cb != b
    offset = (place + 2 * ell) % 4
    chb, cv = place // 2, place % 2
    for rule, name in ((cross & ~other, "q"), (other & ~cross, "r"), (cross & other, "s")):
        for i, (hb, v) in enumerate(order[name]):
            hit = rule & (offset == i)
            chb, cv = jnp.where(hit, hb, chb), jnp.where(hit, v, cv)
    cshift = chb * 16 + cv
    cols = iota((128, 96), 1)
    onehot = jnp.where(cols % 32 == source, 1.0, 0.0).astype(BF16)

    def msg_copy(k, da, dc):
        off = ((k + 1) // 2) * (1 - 2 * (k % 2))
        slot = ((z - off + 8) % 8) * 4 + ((a + da) % 2) * 2 + (c + dc) % 2
        sem = k * 4 + da * 2 + dc
        return pltpu.make_async_remote_copy(
            src_ref=msg.at[slot], dst_ref=rbuf.at[slot], send_sem=msg_send.at[sem],
            recv_sem=msg_recv.at[sem], device_id=dev["d"], device_id_type=MESH,
        )

    def msg_wait(t, _):
        msg_copy(t // 4, (t // 2) % 2, t % 2).wait_recv()
        return 0

    lax.fori_loop(1, 32, msg_wait, 0)
    lane = iota((128, 128), 1)
    kept = (lane < 16) & (lane % 2 == 0)
    near = []
    for f in range(8):
        t = dot(onehot, jnp.concatenate(thirds(rbuf[:, f, :]), axis=0))
        for bit in (64, 32, 16, 1):
            t = jnp.where((cshift // bit) % 2 == 1, pltpu.roll(t, 128 - bit, 1), t)
        there = t > ABSENT / 2
        if f == 0:
            gap = jnp.where(there, 0.0, -3e38)
            for g in range(8):
                pen[g] = gap[:, 2 * g:2 * g + 1]
        t = jnp.where(there & kept, t, 0.0)
        high = t.astype(BF16).astype(F32)
        near.append(high + pltpu.roll(t - high, 16, 1))
    for f in range(8):
        around = pltpu.roll(near[f], 32, 1)
        if f > 0:
            around = around + near[f - 1]
        if f < 7:
            around = around + pltpu.roll(near[f + 1], 64, 1)
        around = around.astype(BF16)
        out = jnp.maximum(dot(jnp.concatenate([around, around], axis=1), w1[...]), 0.0)
        high1, low1 = halves(out)
        for p in range(4):
            x1[p, f + 1, :, 0:128] = high1[:, p * 128:(p + 1) * 128]
            x1[p, f + 1, :, 128:256] = low1[:, p * 128:(p + 1) * 128]

    def second(p, _):
        out = dot(jnp.concatenate([x1[p, i:i + 8].reshape(1024, 256) for i in range(3)], axis=1), w2[...])
        out = jnp.maximum(out[:, :128] + out[:, 128:], 0.0)
        for ref, part in zip((x2h, x2l), halves(out)):
            part = part.reshape(8, 128, 128)
            ref[p + 1, 1:9, :, 0:128] = part
            ref[p, 1:9, :, 128:192] = part[:, :, 0:64]
            ref[p + 2, 1:9, :, 192:256] = part[:, :, 64:128]
        return 0

    lax.fori_loop(0, 4, second, 0)
    scale = jnp.concatenate([out_v[...], out_v[...]], axis=1)
    best[...] = jnp.full((1024, 1), -3e38, F32)

    def third(p, _):
        parts = []
        for i in range(3):
            upper = x2h[p + 1, i:i + 8].reshape(1024, 256)
            parts += [upper, x2l[p + 1, i:i + 8].reshape(1024, 256), upper]
        out = dot(jnp.concatenate(parts, axis=1), w3[...])
        out = jnp.maximum(out, 0.0) * scale
        for s in range(2):
            total = jnp.sum(out[:, s * 128:(s + 1) * 128], axis=1, keepdims=True)
            total = total.reshape(8, 128, 1) + pen[2 * p + s][None]
            best[...] = jnp.maximum(best[...], total.reshape(1024, 1))
        return 0

    lax.fori_loop(0, 4, third, 0)
    mean = jnp.sum(best[...].reshape(8, 128, 1), axis=0) * 0.125
    refined_ref[...] = jnp.sum(
        jnp.where(iota((128, 128), 0) == iota((128, 128), 1), mean, 0.0), axis=0, keepdims=True
    )

    for name, block in (("b", b_r), ("c1", b_q), ("c3", b_s)):
        wait(("coarse", name), cbuf.at[block])
    n, col = iota((128, 256), 0), iota((128, 256), 1)
    ny = (n // 2) % 4
    nxh, nb = (n // 8) % 2, ((ny + 1) // 2) % 2
    want = (nxh * 2 + nb) * 64 + (n // 16) * 8 + (ny // 2) * 2 + n % 2
    scores = pick(jnp.where(col == want, 1.0, 0.0).astype(BF16), cbuf[...].reshape(256, 128))
    relation = (nxh != xh).astype(jnp.int32)[:, :128] + 2 * (nb != b).astype(jnp.int32)[:, :128]
    mine = scores
    for r in range(1, 4):
        mine = jnp.where(relation == r, pltpu.roll(scores, 128 - 32 * r, 1), mine)
    coarse_ref[...] = mine.T[0:4]

    for sent in started:
        sent.wait_send()

    def sent_wait(t, _):
        msg_copy(t // 4, (t // 2) % 2, t % 2).wait_send()
        return 0

    lax.fori_loop(1, 32, sent_wait, 0)


def local(queries, database, db_frames, cand_shard, cand_local, conv_one, conv_two, conv_three, conv_out):
    anywhere = pl.BlockSpec(memory_space=pltpu.HBM)
    vmem = pl.BlockSpec(memory_space=pltpu.VMEM)
    smem = pl.BlockSpec(memory_space=pltpu.SMEM)
    coarse, refined = pl.pallas_call(
        kernel,
        out_shape=(jax.ShapeDtypeStruct((4, 128), F32), jax.ShapeDtypeStruct((1, 128), F32)),
        in_specs=[anywhere, anywhere, smem] + [anywhere] * 6,
        out_specs=(vmem, vmem),
        scratch_shapes=[
            pltpu.VMEM((32, 128, K), BF16),
            pltpu.VMEM((16, 128, K), BF16),
            pltpu.VMEM((4, 256, K), BF16),
            pltpu.VMEM((2, 2, 256, K), BF16),
            pltpu.VMEM((32, 8, 128), F32),
            pltpu.VMEM((4, 8, 128), F32),
            pltpu.VMEM((32, 8, 128), F32),
            pltpu.VMEM((32, 8, 128), F32),
            pltpu.VMEM((4, 8, 8, 128), F32),
            pltpu.VMEM((256, 256), BF16),
            pltpu.VMEM((1, 128), jnp.int32),
            pltpu.VMEM((1, 128), jnp.int32),
            pltpu.VMEM((3, 3, 1, 32), F32),
            pltpu.VMEM((288, 64), F32),
            pltpu.VMEM((576, 128), F32),
            pltpu.VMEM((1, 128), F32),
            pltpu.VMEM((256, 512), BF16),
            pltpu.VMEM((768, 256), BF16),
            pltpu.VMEM((2304, 256), BF16),
            pltpu.VMEM((4, 10, 128, 256), BF16),
            pltpu.VMEM((6, 10, 128, 256), BF16),
            pltpu.VMEM((6, 10, 128, 256), BF16),
            pltpu.VMEM((8, 128, 1), F32),
            pltpu.VMEM((1024, 1), F32),
            pltpu.SemaphoreType.DMA((72,)),
            pltpu.SemaphoreType.DMA((72,)),
            pltpu.SemaphoreType.DMA((32,)),
            pltpu.SemaphoreType.DMA((32,)),
            pltpu.SemaphoreType.DMA((8,)),
        ],
        compiler_params=pltpu.CompilerParams(
            collective_id=0, has_side_effects=True, vmem_limit_bytes=64 * 1024 * 1024
        ),
        cost_estimate=pl.CostEstimate(flops=13_000_000_000, bytes_accessed=2_000_000, transcendentals=0),
    )(
        queries.reshape(128, K), database.reshape(4, 128, K), db_frames, cand_shard.reshape(1, 128),
        cand_local.reshape(1, 128), conv_one, conv_two.reshape(288, 64),
        conv_three.reshape(576, 128), conv_out.reshape(1, 128),
    )
    return coarse.T[None], refined[None]


def solution(mesh):
    in_specs = (
        P("index", "rep", None, None, None),
        P("index", None, None, None),
        P("index"),
        P("index", "rep", None, None),
        P("index", "rep", None),
        P(),
        P(),
        P(),
        P(),
    )
    out_specs = (P("rep", None, "index"), P("index", "rep", None))
    return jax.shard_map(local, mesh=mesh, in_specs=in_specs, out_specs=out_specs, check_vma=False)
```

time: 81.8 us -> 63.3 us (0.77)
  Pallas kernels: 74.5 us -> 60.7 us
  local copies, waits for them, and re-layouts: 6.33 us -> 1.8 us
    pallas_call x1, Pallas kernels: 74.5 us -> 60.7 us  [local(): pl.pallas_call(kernel, out_shape=(jax.ShapeDtypeStruct((4, 128), F32), ja...]
    unnamed x20 -> x6, local copies, waits for them, and re-layouts: 6.32 us -> 1.8 us
where the time goes in v2:
time: 63.3 us; the launch traced here: 63.2 us
  Pallas kernels  60.7 us (96%)
  local copies, waits for them, and re-layouts  1.8 us (3%)
  between operations  0.65 us (1%)
    pallas_call x1, Pallas kernels, local(): pl.pallas_call(kernel, out_shape=(jax.ShapeDtypeStruct((4, 128), F32), ja...  60.7 us
    unnamed x6, local copies, waits for them, and re-layouts  1.8 us

profile of v2, /device:TPU:1, one launch (start us, length us, event | category | flops | bytes accessed | tf_op | source)
XLA Modules:
  0.0 63.2 jit_solution(2069315311908853330)
XLA Ops:
  0.6 60.7 %shard_map.104 = (f32[4,128]{1,0:T(4,128)}, f32[1,128]{1,0:T(1,128)}) custom-call(bf16[128,512]{1,0:T(8,128)(2,1)} %bitcast.15, bf16[4,128,512]{2,1,0:T(8,128)(2,1)} %bitcast.12, s32[4]{0:T(128)} %frames.1, s32[1,128]{1,0:T(1,128)} %bitcast.16, s32[1,128]{1,0:T(1,128)} %bitcast.17, f32[3,3,1,32]{3,2,1,0:T(1,128)} %one_hbm.1, f32[288,64]{1,0:T(8,128)} %bitcast.14, ...), custom_call_target="tpu_custom_call" | custom-call | flops 12999999488 | bytes 2000000 | tf_op jit(solution)/shard_map/pallas_call | solution.py:576
  61.4 0.0 copy-start
  61.4 0.7 %copy-done = f32[4,128]{1,0:T(4,128)S(1)} copy-done((f32[4,128]{1,0:T(4,128)S(1)}, f32[4,128]{1,0:T(4,128)}, u32[]{:S(2)}) %copy-start) | copy-done | bytes 2072
  62.0 0.0 copy-start.1
  62.0 0.6 copy.13
  62.6 0.1 copy-done.1
  62.7 0.5 copy.14
Async XLA Ops:
  61.4 0.7 %copy-start = (f32[4,128]{1,0:T(4,128)S(1)}, f32[4,128]{1,0:T(4,128)}, u32[]{:S(2)}) copy-start(f32[4,128]{1,0:T(4,128)} %get-tuple-element.4) | copy-start | bytes 6148
  62.0 0.6 %copy-start.1 = (f32[1,128]{1,0:T(1,128)S(1)}, f32[1,128]{1,0:T(1,128)}, u32[]{:S(2)}) copy-start(f32[1,128]{1,0:T(1,128)} %get-tuple-element.5) | copy-start | bytes 1540

commit v3 on v2

v3 whole, which is shorter than its diff:
```python
import functools

import jax
import jax.numpy as jnp
from jax import lax
from jax.experimental import pallas as pl
from jax.experimental.pallas import tpu as pltpu
from jax.sharding import PartitionSpec as P

MESH = pl.DeviceIdType.MESH
F32, BF16 = jnp.float32, jnp.bfloat16
ABSENT = -(2.0 ** 100)
K = 512
ORDER = (
    ("permute", 0), ("permute", 1), ("prepare", 0), ("prepare", 1), ("prepare", 2), ("get", "d", (0, 0)),
    ("prepare", 3), ("prepare", 4), ("prepare", 5), ("prepare", 6), ("prepare", 7), ("prepare", 8), ("prepare", 9),
    ("prepare", 10), ("prepare", 11), ("prepare", 12), ("get", "a", 0), ("put", "+", (1, 2)), ("put", "-", (1, 2)),
    ("get", "+", (1, 1)), ("put", "+", (2, 1)), ("put", "a", 2), ("get", "-", (1, 1)), ("put", "-", (2, 1)),
    ("put", "a", 3), ("get", "a", 1), ("put", "d", (0, 1)), ("get", "+", (1, 0)), ("put", "+", (2, 0)),
    ("put", "d", (1, 0)), ("get", "-", (1, 0)), ("put", "-", (2, 0)), ("put", "d", (2, 0)), ("get", "xh", 0),
    ("put", "xl", 0), ("get", "b", 0), ("put", "xh", 4), ("put", "b", 4), ("put", "xl", 1), ("permute", 2),
    ("get", "d", (0, 1)), ("tile", 0, 0), ("get", "d", (1, 0)), ("lengths",), ("get", "d", (2, 0)),
    ("get", "+", (1, 2)), ("put", "+", (2, 2)), ("get", "-", (1, 2)), ("put", "-", (2, 2)), ("get", "xh", 1),
    ("get", "a", 2), ("put", "d", (1, 1)), ("get", "b", 1), ("put", "xh", 5), ("put", "b", 5), ("permute", 3),
    ("tile", 1, 0), ("get", "+", (2, 1)), ("put", "+", (3, 1)), ("put", "a", 4), ("get", "-", (2, 1)),
    ("put", "-", (3, 1)), ("put", "a", 5), ("get", "d", (1, 1)), ("get", "a", 3), ("put", "d", (2, 1)),
    ("tile", 0, 1), ("tile", 1, 1), ("get", "+", (2, 0)), ("put", "+", (3, 0)), ("put", "d", (3, 0)),
    ("get", "-", (2, 0)), ("put", "-", (3, 0)), ("put", "d", (4, 0)), ("get", "d", (2, 1)), ("get", "xl", 0),
    ("get", "xh", 4), ("put", "xh", 2), ("get", "b", 4), ("put", "b", 2), ("permute", 4), ("tile", 0, 2),
    ("tile", 1, 2), ("get", "d", (3, 0)), ("get", "+", (2, 2)), ("put", "+", (3, 2)), ("get", "-", (2, 2)),
    ("put", "-", (3, 2)), ("get", "d", (4, 0)), ("get", "a", 4), ("put", "d", (3, 1)), ("get", "+", (3, 1)),
    ("put", "+", (4, 1)), ("put", "a", 6), ("get", "-", (3, 1)), ("put", "a", 7), ("get", "xl", 1), ("get", "xh", 5),
    ("get", "b", 5), ("permute", 5), ("permute", 6), ("tile", 2, 0), ("tile", 2, 1), ("get", "d", (3, 1)),
    ("get", "a", 5), ("put", "d", (4, 1)), ("get", "+", (3, 0)), ("put", "+", (4, 0)), ("put", "d", (5, 0)),
    ("get", "-", (3, 0)), ("put", "d", (6, 0)), ("tile", 2, 2), ("tile", 0, 3), ("tile", 1, 3), ("tile", 2, 3),
    ("get", "d", (4, 1)), ("get", "+", (3, 2)), ("get", "-", (3, 2)), ("put", "-", (4, 2)), ("get", "d", (5, 0)),
    ("tile", 0, 4), ("get", "xh", 2), ("get", "d", (6, 0)), ("get", "b", 2), ("permute", 7), ("tile", 3, 0),
    ("post", 0), ("get", "+", (4, 1)), ("put", "a", 8), ("get", "a", 6), ("put", "d", (5, 1)), ("tile", 3, 1),
    ("post", 1), ("tile", 3, 2), ("post", 2), ("tile", 3, 3), ("get", "d", (5, 1)), ("get", "a", 7),
    ("put", "d", (6, 1)), ("get", "+", (4, 0)), ("put", "d", (7, 0)), ("post", 3), ("tile", 1, 4), ("tile", 2, 4),
    ("tile", 3, 4), ("get", "d", (6, 1)), ("post", 4), ("get", "-", (4, 2)), ("get", "d", (7, 0)), ("tile", 0, 5),
    ("tile", 1, 5), ("tile", 2, 5), ("tile", 3, 5), ("get", "a", 8), ("put", "d", (7, 1)), ("post", 5),
    ("tile", 0, 6), ("tile", 1, 6), ("tile", 2, 6), ("tile", 3, 6), ("get", "d", (7, 1)), ("post", 6), ("tile", 0, 7),
    ("tile", 1, 7), ("tile", 2, 7), ("tile", 3, 7), ("post", 7),
)


def dot(a, b):
    return jnp.dot(a, b, preferred_element_type=F32)


def iota(shape, axis):
    return lax.broadcasted_iota(jnp.int32, shape, axis)


def halves(x):
    high = x.astype(BF16)
    return high, (x - high.astype(F32)).astype(BF16)


def thirds(x):
    high, rest = x.astype(BF16), None
    rest = x - high.astype(F32)
    mid = rest.astype(BF16)
    return high, mid, (rest - mid.astype(F32)).astype(BF16)


def pick(onehot, x):
    y = dot(onehot, jnp.concatenate(thirds(x), axis=1))
    n = x.shape[1]
    return y[:, :n] + (y[:, n:2 * n] + y[:, 2 * n:])


def kernel(
    q_hbm, db_hbm, frames, shard_hbm, local_hbm, one_hbm, two_hbm, three_hbm, out_hbm,
    coarse_ref, refined_ref,
    qbuf, dbraw, dbp, fmap, lens, msg, rbuf, cbuf, perm,
    shard_v, local_v, one_v, two_v, three_v, out_v,
    w1, w2, w3, x1, x2h, x2l, products, pen,
    send_sem, recv_sem, msg_send, msg_recv, local_sem,
):
    index, rep = lax.axis_index("index"), lax.axis_index("rep")
    c, y, xh, z = index % 2, (index // 2) % 4, (index // 8) % 2, index // 16
    x = xh * 2 + rep
    a, b = y // 2, ((y + 1) // 2) % 2
    ell = rep

    def device(z, x, y, c):
        return (((z * 2 + x // 2) * 4 + y) * 2 + c, x % 2)

    def y_of(a, b):
        return a * 3 + b * (1 - 2 * a)

    me_q = z * 4 + a * 2 + c
    me_b = xh * 2 + b
    b_own, b_q, b_r, b_s = me_b, (1 - xh) * 2 + b, xh * 2 + (1 - b), (1 - xh) * 2 + (1 - b)
    dev = {
        "+": device((z + 1) % 8, x, y, c),
        "-": device((z + 7) % 8, x, y, c),
        "a": device(z, x, 3 - y, c),
        "b": device(z, x, y_of(a, 1 - b), c),
        "d": device(z, x, y, 1 - c),
        "xh": device(z, 3 - x, y, c),
        "xl": device(z, xh * 2 + (1 - rep), y, c),
        "c1": device(z, (1 - xh) * 2 + rep, y, c),
        "c3": device(z, (1 - xh) * 2 + rep, y_of(a, 1 - b), c),
    }

    def row_device(k, da, dc):
        off = ((k + 1) // 2) * (1 - 2 * (k % 2))
        zk, ak, ck = (z + off + 8) % 8, (a + da) % 2, (c + dc) % 2
        return zk, ak, ck, device(zk, x, y_of(ak, b), ck)

    barrier = pltpu.get_barrier_semaphore()
    for target in dev.values():
        pl.semaphore_signal(barrier, inc=1, device_id=target, device_id_type=MESH)

    loads = [
        pltpu.make_async_copy(src, dst, local_sem.at[i])
        for i, (src, dst) in enumerate((
            (q_hbm, qbuf.at[me_q]),
            (db_hbm, dbraw.at[pl.ds(me_b * 4, 4)]),
            (three_hbm, three_v),
            (two_hbm, two_v),
            (one_hbm, one_v),
            (shard_hbm, shard_v),
            (local_hbm, local_v),
            (out_hbm, out_v),
        ))
    ]
    for load in loads:
        load.start()

    row8 = iota((8, 128), 0)
    own_lens = jnp.zeros((8, 128), F32)
    for u in range(4):
        own_lens = jnp.where(row8 == u, frames[u].astype(F32), own_lens)
    lens[me_b] = own_lens

    ids, started = {}, []

    def copy(name, src, dst, target):
        sem = ids.setdefault(name, len(ids))
        return pltpu.make_async_remote_copy(
            src_ref=src, dst_ref=dst, send_sem=send_sem.at[sem], recv_sem=recv_sem.at[sem],
            device_id=target, device_id_type=MESH,
        )

    def send(name, src, dst, target):
        started.append(copy(name, src, dst, target))
        started[-1].start()

    def wait(name, dst):
        copy(name, dst, dst, dev["d"]).wait_recv()

    def z_at(k):
        return (z + ((k + 1) // 2) * (1 - 2 * (k % 2)) + 8) % 8

    def half(zz, aa, h):
        return qbuf.at[zz * 4 + aa * 2 + c, pl.ds(h * 64, 64), :]

    def unit(zz, aa, cc):
        return qbuf.at[zz * 4 + aa * 2 + cc]

    def db_unit(block, u):
        return dbraw.at[block * 4 + u]

    pl.semaphore_wait(barrier, len(dev))

    def ring_send(way, d, item):
        k = 2 * (d - 1) - (1 if way == "+" else 0) if d > 1 else 0
        zz = z_at(k)
        ref = half(zz, 1 - a, 0) if item == 2 else half(zz, a, item)
        src = q_hbm.at[pl.ds(item * 64, 64), :] if d == 1 and item < 2 else ref
        send((way, d, item), src, ref, dev[way])

    def ring_wait(way, d, item):
        zz = z_at(2 * d - (1 if way == "+" else 0))
        wait((way, d, item), half(zz, 1 - a, 0) if item == 2 else half(zz, a, item))

    def db_at(link, position):
        first = {"xh": (2, 3, 1, None, 0, 1), "b": (2, 3, 1, None, 2, 3)}[link]
        block = b_s if position > 3 else b_q if link == "xh" else b_r
        return block, (2 * ell + first[position]) % 4

    def put(link, key):
        name = (link, key)
        if link in "+-":
            ring_send(link, *key)
        elif link == "a":
            if key < 2:
                send(name, q_hbm.at[pl.ds(key * 64, 64), :], half(z, a, key), dev["a"])
            else:
                ref = half(z_at(key - 1), a, 1)
                send(name, ref, ref, dev["a"])
        elif link == "d":
            k, other = key
            ref = unit(z_at(k), 1 - a if other else a, c)
            send(name, ref if k or other else q_hbm, ref, dev["d"])
        elif link == "xl":
            ref = db_unit(b_r if key else b_q, (2 * ell + 2) % 4)
            send(name, ref, ref, dev["xl"])
        elif key > 3:
            ref = db_unit(b_r if link == "xh" else b_q, (2 * ell + key - 2) % 4)
            send(name, ref, ref, dev[link])
        else:
            first = (0, 1, 3) if link == "xh" else (2, 3, 1)
            u = (2 * ell + first[key]) % 4
            send(name, db_hbm.at[u], db_unit(me_b, u), dev[link])

    def get(link, key):
        name = (link, key)
        if link in "+-":
            ring_wait(link, *key)
        elif link == "a":
            wait(name, half(z, 1 - a, key) if key < 2 else half(z_at(key - 1), 1 - a, 1))
        elif link == "d":
            wait(name, unit(z_at(key[0]), 1 - a if key[1] else a, 1 - c))
        elif link == "xl":
            wait(name, db_unit(b_r if key else b_q, 2 * ell))
        else:
            wait(name, db_unit(*db_at(link, key)))

    for link, keys in (
        ("+", ((1, 1),)), ("-", ((1, 1),)), ("a", (0,)), ("+", ((1, 0),)), ("-", ((1, 0),)), ("a", (1,)),
        ("xh", (0,)), ("b", (0,)), ("d", ((0, 0),)), ("xh", (1,)), ("b", (1,)),
    ):
        for key in keys:
            put(link, key)
    for name in ("b", "c1", "c3"):
        send(("len", name), lens.at[me_b], lens.at[me_b], dev[name])

    ri, ci = iota((256, 256), 0), iota((256, 256), 1)
    perm[...] = jnp.where(
        ci == (ri % 2) * 128 + ((ri // 2) % 8) * 16 + ri // 16, 1.0, 0.0
    ).astype(BF16)

    def permute(hb):
        videos = (
            ((b_own, 0), (b_own, 1)), ((b_own, 2), (b_own, 3)),
            (db_at("xh", 0), db_at("b", 0)), (db_at("xh", 1), db_at("b", 1)), (db_at("xh", 4), db_at("b", 4)),
            (db_at("xh", 5), db_at("b", 5)), ((b_q, 2 * ell), (b_r, 2 * ell)), (db_at("xh", 2), db_at("b", 2)),
        )[hb]
        raw = jnp.concatenate([dbraw[block * 4 + u] for block, u in videos], axis=0)
        rows = dot(perm[...], raw).astype(BF16)
        for u in range(16):
            at = (u % 8) * 32 + (hb % 2) * 16
            dbp[hb // 2, u // 8, at:at + 16, :] = rows[u * 16:(u + 1) * 16]

    lane = iota((8, 128), 1)

    def tile(group, k):
        zz = z_at(k)
        left = qbuf[pl.ds(zz * 4, 4)].reshape(512, K)
        top = None
        for t in range(2):
            sim = lax.dot_general(left, dbp[group, t], (((1,), (1,)), ((), ())), preferred_element_type=F32)
            sim = jnp.maximum(sim[:, :128], sim[:, 128:])
            top = sim if top is None else jnp.maximum(top, sim)
        top = jnp.maximum(top, pltpu.roll(top, 64, 1))
        top = jnp.maximum(top, pltpu.roll(top, 32, 1))
        mean = jnp.sum(top.reshape(32, 16, 128), axis=1).reshape(4, 8, 128)
        at = pl.ds(zz * 4, 4)
        if group:
            mean = jnp.where((lane // 32 == group)[None], mean, fmap[at])
        fmap[at] = mean

    order = {
        "own": ((0, 0), (0, 1), (1, 0), (1, 1)),
        "q": ((6, 0), (7, 0), (2, 0), (3, 0)),
        "r": ((6, 1), (7, 1), (2, 1), (3, 1)),
        "s": ((4, 0), (5, 0), (4, 1), (5, 1)),
    }
    blocks = {"own": b_own, "q": b_q, "r": b_r, "s": b_s}

    def unit_of(name, i):
        return i if name == "own" else (2 * ell + i) % 4

    def length_lanes():
        total = jnp.zeros((1, 128), F32)
        lane1 = iota((1, 128), 1)
        for name, places in order.items():
            for i, (hb, v) in enumerate(places):
                value = lens[blocks[name], pl.ds(unit_of(name, i), 1), :]
                total = jnp.where((lane1 // 16 == hb) & (lane1 % 2 == v), value, total)
        return (lane1 % 16 // 2).astype(F32) < total

    def post(k):
        zz = z_at(k)
        rows = jnp.zeros((8, 128), F32)
        for i in range(4):
            maps = fmap[zz * 4 + i] * (K ** -0.5 / 16)
            maps = jnp.where(present, maps, ABSENT)
            msg[zz * 4 + i] = maps
            for shift in (8, 4, 2):
                maps = jnp.maximum(maps, pltpu.roll(maps, 128 - shift, 1))
            rows = jnp.where(row8 == i, jnp.sum(maps, axis=0, keepdims=True), rows)
        cbuf[me_b, zz] = rows
        for da in range(2):
            for dc in range(2):
                zk, ak, ck, target = row_device(k, da, dc)
                slot = zk * 4 + ak * 2 + ck
                if k == 0 and da == 0 and dc == 0:
                    rbuf[me_q] = msg[slot]
                else:
                    sem = k * 4 + da * 2 + dc
                    pltpu.make_async_remote_copy(
                        src_ref=msg.at[slot], dst_ref=rbuf.at[me_q], send_sem=msg_send.at[sem],
                        recv_sem=msg_recv.at[sem], device_id=target, device_id_type=MESH,
                    ).start()

    def third_weights(j):
        zero = jnp.zeros((64, 128), F32)
        taps = [[three_v[(i * 3 + t) * 64:(i * 3 + t + 1) * 64, :] for i in range(3)] for t in range(3)]
        w = []
        for g0, g1, g2 in taps:
            w.append((g0, (g0 + g2 + g1) * 0.5, (g0 + g2 - g1) * 0.5, g2)[j])
        for r, (left, right) in enumerate(((w[1], w[0]), (w[2], w[1]), (zero, w[2]), (w[0], zero))):
            for s, part in enumerate((left, right)):
                high, low = halves(part)
                for at, value in ((0, high), (256, high), (512, low)):
                    at = j * 768 + at + r * 64
                    w3[at:at + 64, s * 128:(s + 1) * 128] = value

    def second_weights(i):
        place = [jnp.where(iota((64, 128), 1) == iota((64, 128), 0) + 64 * s, 1.0, 0.0).astype(BF16) for s in range(2)]
        zero = jnp.zeros((32, 64), F32)
        w = [two_v[(i * 3 + j) * 32:(i * 3 + j + 1) * 32, :] for j in range(3)]
        stacks = (jnp.concatenate(w + [zero], axis=0), jnp.concatenate([zero] + w, axis=0))
        for part in range(2):
            value = sum(dot(halves(stack)[part], where) for stack, where in zip(stacks, place)).astype(BF16)
            for r in range(2):
                w2[i * 256 + r * 128:i * 256 + (r + 1) * 128, part * 128:(part + 1) * 128] = value

    def first_weights(i):
        spread = jnp.where(iota((32, 512), 1) % 32 == iota((32, 512), 0), 1.0, 0.0).astype(BF16)
        j, col = iota((32, 512), 0), iota((32, 512), 1)
        g = (j % 16) // 2
        pos = 2 * (col // 128) - 1 + (col % 128) // 32
        for part in range(2):
            value = jnp.zeros((32, 512), F32)
            for s in range(3):
                line = dot(halves(jnp.broadcast_to(one_v[i, s], (16, 32)))[part], spread)[0:1]
                hit = (g - pos + 1 == s) & (pos >= 0) & (pos < 8) & (j % 2 == 0)
                value = value + jnp.where(hit, line, 0.0)
            w1[part * 128 + i * 32:part * 128 + (i + 1) * 32, :] = value.astype(BF16)
            if i == 0:
                w1[part * 128 + 96:part * 128 + 128, :] = jnp.zeros((32, 512), BF16)

    def clear_ends(ref):
        for p in range(4):
            for f in (0, 9):
                ref[p, f] = jnp.zeros((128, 256), BF16)

    def clear_sides(ref):
        for p in (1, 4):
            ref[p, :, :, 128:256] = jnp.zeros((16, 128, 128), BF16)

    def prepare(i):
        if i == 0:
            for load in (2, 3, 4):
                loads[load].wait()
        (
            *[functools.partial(third_weights, t) for t in range(4)],
            *[functools.partial(second_weights, t) for t in range(3)],
            *[functools.partial(first_weights, t) for t in range(3)],
            functools.partial(clear_ends, x1),
            *[functools.partial(clear_sides, ref) for ref in (x2h, x2l)],
        )[i]()

    present = None
    loads[0].wait()
    loads[1].wait()
    for step, *which in ORDER:
        if step == "lengths":
            for name, block in (("b", b_r), ("c1", b_q), ("c3", b_s)):
                wait(("len", name), lens.at[block])
            present = length_lanes()
        else:
            dict(get=get, put=put, permute=permute, tile=tile, post=post, prepare=prepare)[step](*which)
    ri, ci = iota((128, 128), 0), iota((128, 128), 1)
    where = ri < 0
    for r, (name, places) in enumerate(order.items()):
        for i, (hb, v) in enumerate(places):
            where = where | ((ri == hb * 16 + v) & (ci == r * 32 + unit_of(name, i)))
    sums = cbuf[me_b].reshape(64, 128)
    where = jnp.where(where, 1.0, 0.0).astype(BF16)
    sums = sum(dot(part, where) for part in thirds(sums)) * 0.125
    cbuf[me_b] = sums.reshape(8, 8, 128)
    for name in ("b", "c1", "c3"):
        send(("coarse", name), cbuf.at[me_b], cbuf.at[me_b], dev[name])

    def column(row):
        return jnp.sum(
            jnp.where(iota((128, 128), 0) == iota((128, 128), 1), row.astype(F32), 0.0), axis=1, keepdims=True
        ).astype(jnp.int32)

    for i in (5, 6, 7):
        loads[i].wait()
    shard, place = column(shard_v[...]), column(local_v[...])
    cy = (shard // 2) % 4
    ca, cb = cy // 2, ((cy + 1) // 2) % 2
    source = (shard // 16) * 4 + ca * 2 + shard % 2
    cross, other = ((shard // 8) % 2) != xh, cb != b
    offset = (place + 2 * ell) % 4
    chb, cv = place // 2, place % 2
    for rule, name in ((cross & ~other, "q"), (other & ~cross, "r"), (cross & other, "s")):
        for i, (hb, v) in enumerate(order[name]):
            hit = rule & (offset == i)
            chb, cv = jnp.where(hit, hb, chb), jnp.where(hit, v, cv)
    cshift = chb * 16 + cv
    cols = iota((128, 96), 1)
    onehot = jnp.where(cols % 32 == source, 1.0, 0.0).astype(BF16)

    def msg_copy(k, da, dc):
        off = ((k + 1) // 2) * (1 - 2 * (k % 2))
        slot = ((z - off + 8) % 8) * 4 + ((a + da) % 2) * 2 + (c + dc) % 2
        sem = k * 4 + da * 2 + dc
        return pltpu.make_async_remote_copy(
            src_ref=msg.at[slot], dst_ref=rbuf.at[slot], send_sem=msg_send.at[sem],
            recv_sem=msg_recv.at[sem], device_id=dev["d"], device_id_type=MESH,
        )

    def msg_wait(t, _):
        msg_copy(t // 4, (t // 2) % 2, t % 2).wait_recv()
        return 0

    lax.fori_loop(1, 32, msg_wait, 0)
    lane = iota((128, 128), 1)
    kept = (lane < 16) & (lane % 2 == 0)
    near = []
    for f in range(8):
        t = dot(onehot, jnp.concatenate(thirds(rbuf[:, f, :]), axis=0))
        for bit in (64, 32, 16, 1):
            t = jnp.where((cshift // bit) % 2 == 1, pltpu.roll(t, 128 - bit, 1), t)
        there = t > ABSENT / 2
        if f == 0:
            gap = jnp.where(there, 0.0, -3e38)
            for g in range(8):
                pen[g] = gap[:, 2 * g:2 * g + 1]
        t = jnp.where(there & kept, t, 0.0)
        high = t.astype(BF16).astype(F32)
        near.append(high + pltpu.roll(t - high, 16, 1))
    arounds = []
    for f in range(8):
        around = pltpu.roll(near[f], 32, 1)
        if f > 0:
            around = around + near[f - 1]
        if f < 7:
            around = around + pltpu.roll(near[f + 1], 64, 1)
        arounds.append(around.astype(BF16))
    around = jnp.concatenate(arounds, axis=0)
    out = jnp.maximum(dot(jnp.concatenate([around, around], axis=1), w1[...]), 0.0)
    for at, part in zip((0, 128), halves(out)):
        part = part.reshape(8, 128, 512)
        for p in range(4):
            x1[p, 1:9, :, at:at + 128] = part[:, :, p * 128:(p + 1) * 128]

    for p in range(4):
        out = dot(jnp.concatenate([x1[p, i:i + 8].reshape(1024, 256) for i in range(3)], axis=1), w2[...])
        out = jnp.maximum(out[:, :128] + out[:, 128:], 0.0)
        row = [out[f * 128:(f + 1) * 128] for f in range(8)]
        for pair in range(4):
            d1, d2 = row[2 * pair], row[2 * pair + 1]
            mixes = (
                row[2 * pair - 1] - d2 if pair else -d2, d1 + d2, d2 - d1,
                d1 - row[2 * pair + 2] if pair < 3 else d1,
            )
            for j, mix in enumerate(mixes):
                for ref, part in zip((x2h, x2l), halves(mix)):
                    at = j * 4 + pair
                    ref[p + 1, at, :, 0:128] = part
                    ref[p, at, :, 128:192] = part[:, 0:64]
                    ref[p + 2, at, :, 192:256] = part[:, 64:128]

    scale = jnp.concatenate([out_v[...], out_v[...]], axis=1)
    best = [None, None]

    for p in range(4):
        for j in range(4):
            upper = x2h[p + 1, j * 4:j * 4 + 4].reshape(512, 256)
            lower = x2l[p + 1, j * 4:j * 4 + 4].reshape(512, 256)
            products[p % 2, j] = dot(jnp.concatenate([upper, lower, upper], axis=1), w3[j * 768:(j + 1) * 768, :])
        m0, m1, m2, m3 = (products[p % 2, j] for j in range(4))
        for at, out in enumerate((m0 + m1 + m2, m1 - m2 - m3)):
            out = jnp.maximum(out, 0.0) * scale
            for s in range(2):
                total = jnp.sum(out[:, s * 128:(s + 1) * 128], axis=1, keepdims=True)
                total = total.reshape(4, 128, 1) + pen[2 * p + s][None]
                best[at] = total if best[at] is None else jnp.maximum(best[at], total)
    mean = jnp.sum(best[0] + best[1], axis=0) * 0.125
    refined_ref[...] = jnp.sum(
        jnp.where(iota((128, 128), 0) == iota((128, 128), 1), mean, 0.0), axis=0, keepdims=True
    )

    for name, block in (("b", b_r), ("c1", b_q), ("c3", b_s)):
        wait(("coarse", name), cbuf.at[block])
    n, col = iota((128, 256), 0), iota((128, 256), 1)
    ny = (n // 2) % 4
    nxh, nb = (n // 8) % 2, ((ny + 1) // 2) % 2
    want = (nxh * 2 + nb) * 64 + (n // 16) * 8 + (ny // 2) * 2 + n % 2
    scores = pick(jnp.where(col == want, 1.0, 0.0).astype(BF16), cbuf[...].reshape(256, 128))
    relation = (nxh != xh).astype(jnp.int32)[:, :128] + 2 * (nb != b).astype(jnp.int32)[:, :128]
    mine = scores
    for r in range(1, 4):
        mine = jnp.where(relation == r, pltpu.roll(scores, 128 - 32 * r, 1), mine)
    coarse_ref[...] = mine.T[0:4]

    for sent in started:
        sent.wait_send()

    def sent_wait(t, _):
        msg_copy(t // 4, (t // 2) % 2, t % 2).wait_send()
        return 0

    lax.fori_loop(1, 32, sent_wait, 0)


def local(queries, database, db_frames, cand_shard, cand_local, conv_one, conv_two, conv_three, conv_out):
    anywhere = pl.BlockSpec(memory_space=pltpu.HBM)
    vmem = pl.BlockSpec(memory_space=pltpu.VMEM)
    smem = pl.BlockSpec(memory_space=pltpu.SMEM)
    coarse, refined = pl.pallas_call(
        kernel,
        out_shape=(jax.ShapeDtypeStruct((4, 128), F32), jax.ShapeDtypeStruct((1, 128), F32)),
        in_specs=[anywhere, anywhere, smem] + [anywhere] * 6,
        out_specs=(vmem, vmem),
        scratch_shapes=[
            pltpu.VMEM((32, 128, K), BF16),
            pltpu.VMEM((16, 128, K), BF16),
            pltpu.VMEM((4, 2, 256, K), BF16),
            pltpu.VMEM((32, 8, 128), F32),
            pltpu.VMEM((4, 8, 128), F32),
            pltpu.VMEM((32, 8, 128), F32),
            pltpu.VMEM((32, 8, 128), F32),
            pltpu.VMEM((4, 8, 8, 128), F32),
            pltpu.VMEM((256, 256), BF16),
            pltpu.VMEM((1, 128), jnp.int32),
            pltpu.VMEM((1, 128), jnp.int32),
            pltpu.VMEM((3, 3, 1, 32), F32),
            pltpu.VMEM((288, 64), F32),
            pltpu.VMEM((576, 128), F32),
            pltpu.VMEM((1, 128), F32),
            pltpu.VMEM((256, 512), BF16),
            pltpu.VMEM((768, 256), BF16),
            pltpu.VMEM((3072, 256), BF16),
            pltpu.VMEM((4, 10, 128, 256), BF16),
            pltpu.VMEM((6, 16, 128, 256), BF16),
            pltpu.VMEM((6, 16, 128, 256), BF16),
            pltpu.VMEM((2, 4, 512, 256), F32),
            pltpu.VMEM((8, 128, 1), F32),
            pltpu.SemaphoreType.DMA((72,)),
            pltpu.SemaphoreType.DMA((72,)),
            pltpu.SemaphoreType.DMA((32,)),
            pltpu.SemaphoreType.DMA((32,)),
            pltpu.SemaphoreType.DMA((8,)),
        ],
        compiler_params=pltpu.CompilerParams(
            collective_id=0, has_side_effects=True, vmem_limit_bytes=64 * 1024 * 1024
        ),
        cost_estimate=pl.CostEstimate(flops=13_000_000_000, bytes_accessed=2_000_000, transcendentals=0),
    )(
        queries.reshape(128, K), database.reshape(4, 128, K), db_frames, cand_shard.reshape(1, 128),
        cand_local.reshape(1, 128), conv_one, conv_two.reshape(288, 64),
        conv_three.reshape(576, 128), conv_out.reshape(1, 128),
    )
    return coarse.T[None], refined[None]


def solution(mesh):
    in_specs = (
        P("index", "rep", None, None, None),
        P("index", None, None, None),
        P("index"),
        P("index", "rep", None, None),
        P("index", "rep", None),
        P(),
        P(),
        P(),
        P(),
    )
    out_specs = (P("rep", None, "index"), P("index", "rep", None))
    return jax.shard_map(local, mesh=mesh, in_specs=in_specs, out_specs=out_specs, check_vma=False)
```

time: 63.3 us -> 58.3 us (0.921)
  Pallas kernels: 60.7 us -> 55.7 us
    pallas_call x1, Pallas kernels: 60.7 us -> 55.7 us  [local(): pl.pallas_call(kernel, out_shape=(jax.ShapeDtypeStruct((4, 128), F32), ja...]
where the time goes in v3:
time: 58.3 us; the launch traced here: 58.2 us
  Pallas kernels  55.7 us (96%)
  local copies, waits for them, and re-layouts  1.8 us (3%)
  between operations  0.65 us (1%)
    pallas_call x1, Pallas kernels, local(): pl.pallas_call(kernel, out_shape=(jax.ShapeDtypeStruct((4, 128), F32), ja...  55.7 us
    unnamed x6, local copies, waits for them, and re-layouts  1.8 us

profile of v3, /device:TPU:1, one launch (start us, length us, event | category | flops | bytes accessed | tf_op | source)
XLA Modules:
  0.0 58.2 jit_solution(12179185078033042290)
XLA Ops:
  0.6 55.7 %shard_map.104 = (f32[4,128]{1,0:T(4,128)}, f32[1,128]{1,0:T(1,128)}) custom-call(bf16[128,512]{1,0:T(8,128)(2,1)} %bitcast.15, bf16[4,128,512]{2,1,0:T(8,128)(2,1)} %bitcast.12, s32[4]{0:T(128)} %frames.1, s32[1,128]{1,0:T(1,128)} %bitcast.16, s32[1,128]{1,0:T(1,128)} %bitcast.17, f32[3,3,1,32]{3,2,1,0:T(1,128)} %one_hbm.1, f32[288,64]{1,0:T(8,128)} %bitcast.14, ...), custom_call_target="tpu_custom_call" | custom-call | flops 12999999488 | bytes 2000000 | tf_op jit(solution)/shard_map/pallas_call | solution.py:523
  56.4 0.0 copy-start
  56.4 0.7 %copy-done = f32[4,128]{1,0:T(4,128)S(1)} copy-done((f32[4,128]{1,0:T(4,128)S(1)}, f32[4,128]{1,0:T(4,128)}, u32[]{:S(2)}) %copy-start) | copy-done | bytes 2072
  57.0 0.0 copy-start.1
  57.0 0.6 copy.13
  57.6 0.1 copy-done.1
  57.7 0.5 copy.14
Async XLA Ops:
  56.4 0.7 %copy-start = (f32[4,128]{1,0:T(4,128)S(1)}, f32[4,128]{1,0:T(4,128)}, u32[]{:S(2)}) copy-start(f32[4,128]{1,0:T(4,128)} %get-tuple-element.4) | copy-start | bytes 6148
  57.0 0.6 %copy-start.1 = (f32[1,128]{1,0:T(1,128)S(1)}, f32[1,128]{1,0:T(1,128)}, u32[]{:S(2)}) copy-start(f32[1,128]{1,0:T(1,128)} %get-tuple-element.5) | copy-start | bytes 1540

commit v4 on v3

--- a/solution.py
+++ b/solution.py
@@ -12,36 +12,36 @@
 ABSENT = -(2.0 ** 100)
 K = 512
 ORDER = (
-    ("permute", 0), ("permute", 1), ("prepare", 0), ("prepare", 1), ("prepare", 2), ("get", "d", (0, 0)),
-    ("prepare", 3), ("prepare", 4), ("prepare", 5), ("prepare", 6), ("prepare", 7), ("prepare", 8), ("prepare", 9),
+    ("permute", 0), ("permute", 1), ("prepare", 0), ("prepare", 1), ("prepare", 2), ("prepare", 3), ("prepare", 4),
+    ("get", "d", (0, 0)), ("prepare", 5), ("prepare", 6), ("prepare", 7), ("prepare", 8), ("prepare", 9),
     ("prepare", 10), ("prepare", 11), ("prepare", 12), ("get", "a", 0), ("put", "+", (1, 2)), ("put", "-", (1, 2)),
     ("get", "+", (1, 1)), ("put", "+", (2, 1)), ("put", "a", 2), ("get", "-", (1, 1)), ("put", "-", (2, 1)),
     ("put", "a", 3), ("get", "a", 1), ("put", "d", (0, 1)), ("get", "+", (1, 0)), ("put", "+", (2, 0)),
     ("put", "d", (1, 0)), ("get", "-", (1, 0)), ("put", "-", (2, 0)), ("put", "d", (2, 0)), ("get", "xh", 0),
     ("put", "xl", 0), ("get", "b", 0), ("put", "xh", 4), ("put", "b", 4), ("put", "xl", 1), ("permute", 2),
-    ("get", "d", (0, 1)), ("tile", 0, 0), ("get", "d", (1, 0)), ("lengths",), ("get", "d", (2, 0)),
+    ("get", "d", (0, 1)), ("tile", 0, 0), ("get", "d", (1, 0)), ("get", "d", (2, 0)),
     ("get", "+", (1, 2)), ("put", "+", (2, 2)), ("get", "-", (1, 2)), ("put", "-", (2, 2)), ("get", "xh", 1),
     ("get", "a", 2), ("put", "d", (1, 1)), ("get", "b", 1), ("put", "xh", 5), ("put", "b", 5), ("permute", 3),
     ("tile", 1, 0), ("get", "+", (2, 1)), ("put", "+", (3, 1)), ("put", "a", 4), ("get", "-", (2, 1)),
-    ("put", "-", (3, 1)), ("put", "a", 5), ("get", "d", (1, 1)), ("get", "a", 3), ("put", "d", (2, 1)),
+    ("put", "-", (3, 1)), ("put", "a", 5), ("get", "a", 3), ("put", "d", (2, 1)), ("get", "d", (1, 1)),
     ("tile", 0, 1), ("tile", 1, 1), ("get", "+", (2, 0)), ("put", "+", (3, 0)), ("put", "d", (3, 0)),
     ("get", "-", (2, 0)), ("put", "-", (3, 0)), ("put", "d", (4, 0)), ("get", "d", (2, 1)), ("get", "xl", 0),
-    ("get", "xh", 4), ("put", "xh", 2), ("get", "b", 4), ("put", "b", 2), ("permute", 4), ("tile", 0, 2),
-    ("tile", 1, 2), ("get", "d", (3, 0)), ("get", "+", (2, 2)), ("put", "+", (3, 2)), ("get", "-", (2, 2)),
-    ("put", "-", (3, 2)), ("get", "d", (4, 0)), ("get", "a", 4), ("put", "d", (3, 1)), ("get", "+", (3, 1)),
-    ("put", "+", (4, 1)), ("put", "a", 6), ("get", "-", (3, 1)), ("put", "a", 7), ("get", "xl", 1), ("get", "xh", 5),
-    ("get", "b", 5), ("permute", 5), ("permute", 6), ("tile", 2, 0), ("tile", 2, 1), ("get", "d", (3, 1)),
-    ("get", "a", 5), ("put", "d", (4, 1)), ("get", "+", (3, 0)), ("put", "+", (4, 0)), ("put", "d", (5, 0)),
-    ("get", "-", (3, 0)), ("put", "d", (6, 0)), ("tile", 2, 2), ("tile", 0, 3), ("tile", 1, 3), ("tile", 2, 3),
-    ("get", "d", (4, 1)), ("get", "+", (3, 2)), ("get", "-", (3, 2)), ("put", "-", (4, 2)), ("get", "d", (5, 0)),
-    ("tile", 0, 4), ("get", "xh", 2), ("get", "d", (6, 0)), ("get", "b", 2), ("permute", 7), ("tile", 3, 0),
-    ("post", 0), ("get", "+", (4, 1)), ("put", "a", 8), ("get", "a", 6), ("put", "d", (5, 1)), ("tile", 3, 1),
-    ("post", 1), ("tile", 3, 2), ("post", 2), ("tile", 3, 3), ("get", "d", (5, 1)), ("get", "a", 7),
-    ("put", "d", (6, 1)), ("get", "+", (4, 0)), ("put", "d", (7, 0)), ("post", 3), ("tile", 1, 4), ("tile", 2, 4),
-    ("tile", 3, 4), ("get", "d", (6, 1)), ("post", 4), ("get", "-", (4, 2)), ("get", "d", (7, 0)), ("tile", 0, 5),
-    ("tile", 1, 5), ("tile", 2, 5), ("tile", 3, 5), ("get", "a", 8), ("put", "d", (7, 1)), ("post", 5),
-    ("tile", 0, 6), ("tile", 1, 6), ("tile", 2, 6), ("tile", 3, 6), ("get", "d", (7, 1)), ("post", 6), ("tile", 0, 7),
-    ("tile", 1, 7), ("tile", 2, 7), ("tile", 3, 7), ("post", 7),
+    ("tile", 0, 2), ("get", "xh", 4), ("put", "xh", 2), ("get", "b", 4), ("put", "b", 2), ("permute", 4),
+    ("get", "d", (3, 0)), ("get", "+", (2, 2)), ("put", "+", (3, 2)), ("get", "-", (2, 2)), ("put", "-", (3, 2)),
+    ("get", "d", (4, 0)), ("tile", 1, 2), ("get", "+", (3, 1)), ("put", "+", (4, 1)), ("put", "a", 6),
+    ("get", "a", 4), ("put", "d", (3, 1)), ("get", "-", (3, 1)), ("put", "g", 1), ("put", "a", 7), ("get", "xl", 1),
+    ("get", "xh", 5), ("get", "b", 5), ("permute", 5), ("permute", 6), ("tile", 2, 2), ("get", "+", (3, 0)),
+    ("put", "+", (4, 0)), ("put", "d", (5, 0)), ("get", "a", 5), ("put", "d", (4, 1)), ("get", "d", (3, 1)),
+    ("get", "-", (3, 0)), ("put", "g", 0), ("put", "d", (6, 0)), ("tile", 0, 3), ("tile", 1, 3), ("tile", 2, 3),
+    ("get", "+", (3, 2)), ("get", "d", (5, 0)), ("get", "-", (3, 2)), ("get", "d", (4, 1)), ("get", "d", (6, 0)),
+    ("tile", 0, 4), ("get", "xh", 2), ("get", "b", 2), ("permute", 7), ("get", "a", 6), ("put", "d", (5, 1)),
+    ("get", "+", (4, 1)), ("tile", 1, 4), ("tile", 2, 4), ("tile", 3, 4), ("lengths",), ("post", 4), ("get", "g", 1),
+    ("get", "d", (5, 1)), ("get", "+", (4, 0)), ("put", "d", (7, 0)), ("tile", 0, 5), ("tile", 1, 5), ("tile", 2, 5),
+    ("tile", 3, 5), ("get", "a", 7), ("put", "d", (6, 1)), ("get", "d", (7, 0)), ("get", "g", 0),
+    ("put", "d", (7, 1)), ("post", 5), ("tile", 3, 3), ("post", 3), ("tile", 3, 2), ("post", 2), ("get", "d", (6, 1)),
+    ("tile", 0, 6), ("get", "d", (7, 1)), ("tile", 0, 7), ("tile", 1, 7), ("tile", 2, 7), ("tile", 3, 7), ("post", 7),
+    ("tile", 1, 6), ("tile", 2, 6), ("tile", 3, 6), ("post", 6), ("tile", 2, 1), ("tile", 3, 1), ("post", 1),
+    ("tile", 2, 0), ("tile", 3, 0), ("post", 0),
 )
 
 
@@ -73,7 +73,7 @@
 
 def kernel(
     q_hbm, db_hbm, frames, shard_hbm, local_hbm, one_hbm, two_hbm, three_hbm, out_hbm,
-    coarse_ref, refined_ref,
+    out_ref,
     qbuf, dbraw, dbp, fmap, lens, msg, rbuf, cbuf, perm,
     shard_v, local_v, one_v, two_v, three_v, out_v,
     w1, w2, w3, x1, x2h, x2l, products, pen,
@@ -102,13 +102,16 @@
         "d": device(z, x, y, 1 - c),
         "xh": device(z, 3 - x, y, c),
         "xl": device(z, xh * 2 + (1 - rep), y, c),
+    }
+    far = {
         "c1": device(z, (1 - xh) * 2 + rep, y, c),
         "c3": device(z, (1 - xh) * 2 + rep, y_of(a, 1 - b), c),
     }
 
+    diagonal = device((z + 7) % 8, x, 3 - y, c)
+
     def row_device(k, da, dc):
-        off = ((k + 1) // 2) * (1 - 2 * (k % 2))
-        zk, ak, ck = (z + off + 8) % 8, (a + da) % 2, (c + dc) % 2
+        zk, ak, ck = z_at(k), 1 - a if da else a, 1 - c if dc else c
         return zk, ak, ck, device(zk, x, y_of(ak, b), ck)
 
     barrier = pltpu.get_barrier_semaphore()
@@ -153,8 +156,10 @@
     def wait(name, dst):
         copy(name, dst, dst, dev["d"]).wait_recv()
 
+    around_z = [(z + ((k + 1) // 2) * (1 - 2 * (k % 2)) + 8) % 8 for k in range(9)]
+
     def z_at(k):
-        return (z + ((k + 1) // 2) * (1 - 2 * (k % 2)) + 8) % 8
+        return around_z[k]
 
     def half(zz, aa, h):
         return qbuf.at[zz * 4 + aa * 2 + c, pl.ds(h * 64, 64), :]
@@ -197,6 +202,9 @@
             k, other = key
             ref = unit(z_at(k), 1 - a if other else a, c)
             send(name, ref if k or other else q_hbm, ref, dev["d"])
+        elif link == "g":
+            ref = half(z_at(6), a, key)
+            send(name, ref, ref, diagonal)
         elif link == "xl":
             ref = db_unit(b_r if key else b_q, (2 * ell + 2) % 4)
             send(name, ref, ref, dev["xl"])
@@ -216,6 +224,8 @@
             wait(name, half(z, 1 - a, key) if key < 2 else half(z_at(key - 1), 1 - a, 1))
         elif link == "d":
             wait(name, unit(z_at(key[0]), 1 - a if key[1] else a, 1 - c))
+        elif link == "g":
+            wait(name, half(z_at(7), 1 - a, key))
         elif link == "xl":
             wait(name, db_unit(b_r if key else b_q, 2 * ell))
         else:
@@ -227,8 +237,7 @@
     ):
         for key in keys:
             put(link, key)
-    for name in ("b", "c1", "c3"):
-        send(("len", name), lens.at[me_b], lens.at[me_b], dev[name])
+    send(("len", "b"), lens.at[me_b], lens.at[me_b], dev["b"])
 
     ri, ci = iota((256, 256), 0), iota((256, 256), 1)
     perm[...] = jnp.where(
@@ -260,10 +269,7 @@
         top = jnp.maximum(top, pltpu.roll(top, 64, 1))
         top = jnp.maximum(top, pltpu.roll(top, 32, 1))
         mean = jnp.sum(top.reshape(32, 16, 128), axis=1).reshape(4, 8, 128)
-        at = pl.ds(zz * 4, 4)
-        if group:
-            mean = jnp.where((lane // 32 == group)[None], mean, fmap[at])
-        fmap[at] = mean
+        fmap[group, pl.ds(zz * 4, 4)] = mean
 
     order = {
         "own": ((0, 0), (0, 1), (1, 0), (1, 1)),
@@ -289,7 +295,10 @@
         zz = z_at(k)
         rows = jnp.zeros((8, 128), F32)
         for i in range(4):
-            maps = fmap[zz * 4 + i] * (K ** -0.5 / 16)
+            maps = fmap[0, zz * 4 + i]
+            for group in range(1, 4):
+                maps = jnp.where(lane // 32 == group, fmap[group, zz * 4 + i], maps)
+            maps = maps * (K ** -0.5 / 16)
             maps = jnp.where(present, maps, ABSENT)
             msg[zz * 4 + i] = maps
             for shift in (8, 4, 2):
@@ -303,10 +312,9 @@
                 if k == 0 and da == 0 and dc == 0:
                     rbuf[me_q] = msg[slot]
                 else:
-                    sem = k * 4 + da * 2 + dc
                     pltpu.make_async_remote_copy(
-                        src_ref=msg.at[slot], dst_ref=rbuf.at[me_q], send_sem=msg_send.at[sem],
-                        recv_sem=msg_recv.at[sem], device_id=target, device_id_type=MESH,
+                        src_ref=msg.at[slot], dst_ref=rbuf.at[me_q], send_sem=msg_send.at[0],
+                        recv_sem=msg_recv.at[0], device_id=target, device_id_type=MESH,
                     ).start()
 
     def third_weights(j):
@@ -378,6 +386,9 @@
             present = length_lanes()
         else:
             dict(get=get, put=put, permute=permute, tile=tile, post=post, prepare=prepare)[step](*which)
+        if (step, *which) == ("get", "xh", 4):
+            for name in ("c1", "c3"):
+                send(("len", name), lens.at[me_b], lens.at[me_b], far[name])
     ri, ci = iota((128, 128), 0), iota((128, 128), 1)
     where = ri < 0
     for r, (name, places) in enumerate(order.items()):
@@ -388,7 +399,7 @@
     sums = sum(dot(part, where) for part in thirds(sums)) * 0.125
     cbuf[me_b] = sums.reshape(8, 8, 128)
     for name in ("b", "c1", "c3"):
-        send(("coarse", name), cbuf.at[me_b], cbuf.at[me_b], dev[name])
+        send(("coarse", name), cbuf.at[me_b], cbuf.at[me_b], (dev | far)[name])
 
     def column(row):
         return jnp.sum(
@@ -412,20 +423,14 @@
     cols = iota((128, 96), 1)
     onehot = jnp.where(cols % 32 == source, 1.0, 0.0).astype(BF16)
 
-    def msg_copy(k, da, dc):
-        off = ((k + 1) // 2) * (1 - 2 * (k % 2))
-        slot = ((z - off + 8) % 8) * 4 + ((a + da) % 2) * 2 + (c + dc) % 2
-        sem = k * 4 + da * 2 + dc
-        return pltpu.make_async_remote_copy(
-            src_ref=msg.at[slot], dst_ref=rbuf.at[slot], send_sem=msg_send.at[sem],
-            recv_sem=msg_recv.at[sem], device_id=dev["d"], device_id_type=MESH,
-        )
-
-    def msg_wait(t, _):
-        msg_copy(t // 4, (t // 2) % 2, t % 2).wait_recv()
-        return 0
-
-    lax.fori_loop(1, 32, msg_wait, 0)
+    for sent in started:
+        sent.wait_send()
+    messages = pltpu.make_async_remote_copy(
+        src_ref=msg.at[pl.ds(0, 31)], dst_ref=rbuf.at[pl.ds(0, 31)], send_sem=msg_send.at[0],
+        recv_sem=msg_recv.at[0], device_id=dev["d"], device_id_type=MESH,
+    )
+    messages.wait_send()
+    messages.wait_recv()
     lane = iota((128, 128), 1)
     kept = (lane < 16) & (lane % 2 == 0)
     near = []
@@ -489,7 +494,7 @@
                 total = total.reshape(4, 128, 1) + pen[2 * p + s][None]
                 best[at] = total if best[at] is None else jnp.maximum(best[at], total)
     mean = jnp.sum(best[0] + best[1], axis=0) * 0.125
-    refined_ref[...] = jnp.sum(
+    out_ref[4:5, :] = jnp.sum(
         jnp.where(iota((128, 128), 0) == iota((128, 128), 1), mean, 0.0), axis=0, keepdims=True
     )
 
@@ -504,32 +509,28 @@
     mine = scores
     for r in range(1, 4):
         mine = jnp.where(relation == r, pltpu.roll(scores, 128 - 32 * r, 1), mine)
-    coarse_ref[...] = mine.T[0:4]
-
-    for sent in started:
-        sent.wait_send()
-
-    def sent_wait(t, _):
-        msg_copy(t // 4, (t // 2) % 2, t % 2).wait_send()
-        return 0
-
-    lax.fori_loop(1, 32, sent_wait, 0)
+    out_ref[0:4, :] = mine.T[0:4]
+
+
+def split_rows(scores_ref, coarse_ref, refined_ref):
+    coarse_ref[...] = scores_ref[0:4, :]
+    refined_ref[...] = scores_ref[4:5, :]
 
 
 def local(queries, database, db_frames, cand_shard, cand_local, conv_one, conv_two, conv_three, conv_out):
     anywhere = pl.BlockSpec(memory_space=pltpu.HBM)
     vmem = pl.BlockSpec(memory_space=pltpu.VMEM)
     smem = pl.BlockSpec(memory_space=pltpu.SMEM)
-    coarse, refined = pl.pallas_call(
+    scores = pl.pallas_call(
         kernel,
-        out_shape=(jax.ShapeDtypeStruct((4, 128), F32), jax.ShapeDtypeStruct((1, 128), F32)),
+        out_shape=jax.ShapeDtypeStruct((8, 128), F32),
         in_specs=[anywhere, anywhere, smem] + [anywhere] * 6,
-        out_specs=(vmem, vmem),
+        out_specs=vmem,
         scratch_shapes=[
             pltpu.VMEM((32, 128, K), BF16),
             pltpu.VMEM((16, 128, K), BF16),
             pltpu.VMEM((4, 2, 256, K), BF16),
-            pltpu.VMEM((32, 8, 128), F32),
+            pltpu.VMEM((4, 32, 8, 128), F32),
             pltpu.VMEM((4, 8, 128), F32),
             pltpu.VMEM((32, 8, 128), F32),
             pltpu.VMEM((32, 8, 128), F32),
@@ -551,8 +552,8 @@
             pltpu.VMEM((8, 128, 1), F32),
             pltpu.SemaphoreType.DMA((72,)),
             pltpu.SemaphoreType.DMA((72,)),
-            pltpu.SemaphoreType.DMA((32,)),
-            pltpu.SemaphoreType.DMA((32,)),
+            pltpu.SemaphoreType.DMA((1,)),
+            pltpu.SemaphoreType.DMA((1,)),
             pltpu.SemaphoreType.DMA((8,)),
         ],
         compiler_params=pltpu.CompilerParams(
@@ -564,6 +565,10 @@
         cand_local.reshape(1, 128), conv_one, conv_two.reshape(288, 64),
         conv_three.reshape(576, 128), conv_out.reshape(1, 128),
     )
+    coarse, refined = pl.pallas_call(
+        split_rows,
+        out_shape=(jax.ShapeDtypeStruct((4, 128), F32), jax.ShapeDtypeStruct((1, 128), F32)),
+    )(scores)
     return coarse.T[None], refined[None]
 
 

time: 58.3 us -> 56.7 us (0.973)
  local copies, waits for them, and re-layouts: 1.8 us -> 0 us
    unnamed x6 -> x0, local copies, waits for them, and re-layouts: 1.8 us -> none
    pallas_call x1 -> x2, Pallas kernels: 55.7 us -> 56 us  [the longest x1 54.7 us: local(): pl.pallas_call(kernel, out_shape=jax.ShapeDtypeStruct((8, 128), F32), in_...]
where the time goes in v4:
time: 56.7 us; the launch traced here: 56.6 us
  Pallas kernels  56 us (99%)
  between operations  0.64 us (1%)
    pallas_call x1, Pallas kernels, local(): pl.pallas_call(kernel, out_shape=jax.ShapeDtypeStruct((8, 128), F32), in_...  54.7 us
    pallas_call x1, Pallas kernels, local(): pl.pallas_call(split_rows, out_shape=(jax.ShapeDtypeStruct((4, 128), F32)...  1.25 us

profile of v4, /device:TPU:1, one launch (start us, length us, event | category | flops | bytes accessed | tf_op | source)
XLA Modules:
  0.0 56.6 jit_solution(17906292347941871283)
XLA Ops:
  0.6 54.7 %shard_map.104.scores_ref = f32[8,128]{1,0:T(8,128)} custom-call(bf16[128,512]{1,0:T(8,128)(2,1)} %bitcast.14, bf16[4,128,512]{2,1,0:T(8,128)(2,1)} %bitcast.11, s32[4]{0:T(128)} %frames.1, s32[1,128]{1,0:T(1,128)} %bitcast.16, s32[1,128]{1,0:T(1,128)} %bitcast.17, f32[3,3,1,32]{3,2,1,0:T(1,128)} %one_hbm.1, f32[288,64]{1,0:T(8,128)} %bitcast.13, ...), custom_call_target="tpu_custom_call" | custom-call | flops 12999999488 | bytes 2000000 | tf_op jit(solution)/shard_map/pallas_call | solution.py:524
  55.4 1.3 %shard_map.105 = (f32[4,128]{1,0:T(4,128)}, f32[1,128]{1,0:T(1,128)}) custom-call(f32[8,128]{1,0:T(8,128)} %shard_map.104.scores_ref), custom_call_target="tpu_custom_call" | custom-call | tf_op jit(solution)/shard_map/pallas_call | solution.py:568

commit v5 on v4

--- a/solution.py
+++ b/solution.py
@@ -293,18 +293,14 @@
 
     def post(k):
         zz = z_at(k)
-        rows = jnp.zeros((8, 128), F32)
+        found = []
         for i in range(4):
             maps = fmap[0, zz * 4 + i]
             for group in range(1, 4):
                 maps = jnp.where(lane // 32 == group, fmap[group, zz * 4 + i], maps)
-            maps = maps * (K ** -0.5 / 16)
-            maps = jnp.where(present, maps, ABSENT)
+            maps = jnp.where(present, maps * (K ** -0.5 / 16), ABSENT)
             msg[zz * 4 + i] = maps
-            for shift in (8, 4, 2):
-                maps = jnp.maximum(maps, pltpu.roll(maps, 128 - shift, 1))
-            rows = jnp.where(row8 == i, jnp.sum(maps, axis=0, keepdims=True), rows)
-        cbuf[me_b, zz] = rows
+            found.append(maps)
         for da in range(2):
             for dc in range(2):
                 zk, ak, ck, target = row_device(k, da, dc)
@@ -316,6 +312,12 @@
                         src_ref=msg.at[slot], dst_ref=rbuf.at[me_q], send_sem=msg_send.at[0],
                         recv_sem=msg_recv.at[0], device_id=target, device_id_type=MESH,
                     ).start()
+        rows = jnp.zeros((8, 128), F32)
+        for i, maps in enumerate(found):
+            for shift in (8, 4, 2):
+                maps = jnp.maximum(maps, pltpu.roll(maps, 128 - shift, 1))
+            rows = jnp.where(row8 == i, jnp.sum(maps, axis=0, keepdims=True), rows)
+        cbuf[me_b, zz] = rows
 
     def third_weights(j):
         zero = jnp.zeros((64, 128), F32)
@@ -431,6 +433,8 @@
     )
     messages.wait_send()
     messages.wait_recv()
+    for name, block in (("b", b_r), ("c1", b_q), ("c3", b_s)):
+        wait(("coarse", name), cbuf.at[block])
     lane = iota((128, 128), 1)
     kept = (lane < 16) & (lane % 2 == 0)
     near = []
@@ -498,8 +502,6 @@
         jnp.where(iota((128, 128), 0) == iota((128, 128), 1), mean, 0.0), axis=0, keepdims=True
     )
 
-    for name, block in (("b", b_r), ("c1", b_q), ("c3", b_s)):
-        wait(("coarse", name), cbuf.at[block])
     n, col = iota((128, 256), 0), iota((128, 256), 1)
     ny = (n // 2) % 4
     nxh, nb = (n // 8) % 2, ((ny + 1) // 2) % 2

time: 56.7 us -> 55.8 us (0.984)
  Pallas kernels: 56 us -> 55 us
    pallas_call x1, Pallas kernels: 54.7 us -> 53.7 us  [local(): pl.pallas_call(kernel, out_shape=jax.ShapeDtypeStruct((8, 128), F32), in_...]
where the time goes in v5:
time: 55.8 us; the launch traced here: 55.6 us
  Pallas kernels  55 us (99%)
  between operations  0.64 us (1%)
    pallas_call x1, Pallas kernels, local(): pl.pallas_call(kernel, out_shape=jax.ShapeDtypeStruct((8, 128), F32), in_...  53.7 us
    pallas_call x1, Pallas kernels, local(): pl.pallas_call(split_rows, out_shape=(jax.ShapeDtypeStruct((4, 128), F32)...  1.25 us

profile of v5, /device:TPU:1, one launch (start us, length us, event | category | flops | bytes accessed | tf_op | source)
XLA Modules:
  0.0 55.6 jit_solution(7456907534808122028)
XLA Ops:
  0.6 53.7 %shard_map.104.scores_ref = f32[8,128]{1,0:T(8,128)} custom-call(bf16[128,512]{1,0:T(8,128)(2,1)} %bitcast.14, bf16[4,128,512]{2,1,0:T(8,128)(2,1)} %bitcast.11, s32[4]{0:T(128)} %frames.1, s32[1,128]{1,0:T(1,128)} %bitcast.16, s32[1,128]{1,0:T(1,128)} %bitcast.17, f32[3,3,1,32]{3,2,1,0:T(1,128)} %one_hbm.1, f32[288,64]{1,0:T(8,128)} %bitcast.13, ...), custom_call_target="tpu_custom_call" | custom-call | flops 12999999488 | bytes 2000000 | tf_op jit(solution)/shard_map/pallas_call | solution.py:526
  54.4 1.3 %shard_map.105 = (f32[4,128]{1,0:T(4,128)}, f32[1,128]{1,0:T(1,128)}) custom-call(f32[8,128]{1,0:T(8,128)} %shard_map.104.scores_ref), custom_call_target="tpu_custom_call" | custom-call | tf_op jit(solution)/shard_map/pallas_call | solution.py:570

commit v6 on v5

--- a/solution.py
+++ b/solution.py
@@ -301,8 +301,8 @@
             maps = jnp.where(present, maps * (K ** -0.5 / 16), ABSENT)
             msg[zz * 4 + i] = maps
             found.append(maps)
-        for da in range(2):
-            for dc in range(2):
+        for da in (1, 0):
+            for dc in (1, 0):
                 zk, ak, ck, target = row_device(k, da, dc)
                 slot = zk * 4 + ak * 2 + ck
                 if k == 0 and da == 0 and dc == 0:

time: 55.8 us -> 55.4 us (level)
  no operation moved by 1% of the time
where the time goes in v6:
time: 55.4 us; the launch traced here: 55.2 us
  Pallas kernels  54.6 us (99%)
  between operations  0.64 us (1%)
    pallas_call x1, Pallas kernels, local(): pl.pallas_call(kernel, out_shape=jax.ShapeDtypeStruct((8, 128), F32), in_...  53.3 us
    pallas_call x1, Pallas kernels, local(): pl.pallas_call(split_rows, out_shape=(jax.ShapeDtypeStruct((4, 128), F32)...  1.25 us

profile of v6, /device:TPU:1, one launch (start us, length us, event | category | flops | bytes accessed | tf_op | source)
XLA Modules:
  0.0 55.2 jit_solution(16478189136974151187)
XLA Ops:
  0.6 53.3 %shard_map.104.scores_ref = f32[8,128]{1,0:T(8,128)} custom-call(bf16[128,512]{1,0:T(8,128)(2,1)} %bitcast.14, bf16[4,128,512]{2,1,0:T(8,128)(2,1)} %bitcast.11, s32[4]{0:T(128)} %frames.1, s32[1,128]{1,0:T(1,128)} %bitcast.16, s32[1,128]{1,0:T(1,128)} %bitcast.17, f32[3,3,1,32]{3,2,1,0:T(1,128)} %one_hbm.1, f32[288,64]{1,0:T(8,128)} %bitcast.13, ...), custom_call_target="tpu_custom_call" | custom-call | flops 12999999488 | bytes 2000000 | tf_op jit(solution)/shard_map/pallas_call | solution.py:526
  54.0 1.3 %shard_map.105 = (f32[4,128]{1,0:T(4,128)}, f32[1,128]{1,0:T(1,128)}) custom-call(f32[8,128]{1,0:T(8,128)} %shard_map.104.scores_ref), custom_call_target="tpu_custom_call" | custom-call | tf_op jit(solution)/shard_map/pallas_call | solution.py:570
